TPU v7x, 512 devices: a whole 4x8x8 slice. The times are simulated.
512 devices in a mesh: wide: 64 (over y, x, core), narrow: 8 (over z).
Axes of the slice: x: 4, y: 8, z: 8, core: 2. Of those that a mesh axis runs over, the one named last changes fastest.
Arguments:
- base: float32 [2, 192, 192, 192], P(None, 'wide', 'narrow'), may hold values from -6 to 6
- fine_psi: float32 [2048, 2, 16, 256], P(('wide', 'narrow')), may hold values from -6 to 6
- counts: int32 [512], P(('wide', 'narrow')), may hold values from 1 to 4, as said below
- neighbors: int32 [2048, 6], P(('wide', 'narrow')), may hold values from -1 to 2047, as said below
- base_cell: int32 [2048, 6, 3], replicated, may hold values from 0 to 191, as said below
Outputs:
- drifted: float32 [2, 192, 192, 192], P(None, 'wide', 'narrow')
- fine_out: float32 [2048, 2, 16, 256], P(('wide', 'narrow'))
Inputs may be any that keep to these rules, and one draw needn't show every extreme that they name: Each device's live slots are its first counts entries. `neighbors`: A present neighbour is a live slot (device * 4 + slot) of the same device or of the device just before or after it in the order of wide+narrow, wrapping around; faces 2k and 2k + 1 are the lower and upper faces along grid dimension k; padded slots hold -1 everywhere. `base_cell`: the base cell just outside the centre of each face of the group.
All inputs are finite; a program needn't handle non-finite values.
Results may differ from a plain program's by a relative error of at most 0.00024.
Values sent between devices are 32-bit elements; how exact they have to be, the bound alone decides.
No kernel may reach another device: no remote copies, remote signals or barrier semaphores. Data moves between devices by JAX's collectives and lax.ppermute only.
A program may use at most 64 MiB of HBM per device.

v0:
```python
import jax
import jax.numpy as jnp
from jax import lax
from jax.sharding import PartitionSpec as P

SUBCYCLES = 2


PHASE_RATE = 8.0
TAYLOR_STEP = 0.6
EINSUM_FORMS = ("kn,nbc->kbc", "kn,anc->akc", "kn,abn->abk")


def shifted(block, axis, distance):
    devices = range(lax.axis_size(axis))
    route = [((i - distance) % len(devices), i) for i in devices]
    return lax.ppermute(block, axis, route)


def taylor_matrix():
    position = jnp.arange(24)
    offset = position[:, None] - position[None, :]
    laplace = jnp.where(offset == 0, -2.0, 0.0) + jnp.where(jnp.abs(offset) == 1, 1.0, 0.0)
    laplace = laplace.astype(jnp.float32)
    squared = jnp.dot(laplace, laplace, precision=lax.Precision.HIGHEST)
    cubed = jnp.dot(squared, laplace, precision=lax.Precision.HIGHEST)
    fourth = jnp.dot(squared, squared, precision=lax.Precision.HIGHEST)
    identity = jnp.eye(24, dtype=jnp.float32)
    real_full = identity - TAYLOR_STEP**2 / 2.0 * squared + TAYLOR_STEP**4 / 24.0 * fourth
    imag_full = TAYLOR_STEP * laplace - TAYLOR_STEP**3 / 6.0 * cubed
    real_rows = real_full[4:20]
    imag_rows = imag_full[4:20]
    return jnp.concatenate(
        [jnp.concatenate([real_rows, -imag_rows], 1), jnp.concatenate([imag_rows, real_rows], 1)], 0
    )


def rotation_angles(length):
    frequency = jnp.arange(length, dtype=jnp.int32)
    signed_freq = jnp.where(frequency < length // 2, frequency, frequency - length)
    wavenumber = 2.0 * jnp.pi / length * signed_freq.astype(jnp.float32)
    return PHASE_RATE * wavenumber * wavenumber


def dft_tables(length, inverse):
    frequency = jnp.arange(length, dtype=jnp.int32)
    products = frequency[:, None] * frequency[None, :] % length
    angles = 2.0 * jnp.pi / length * products.astype(jnp.float32)
    if inverse:
        return (jnp.cos(angles) / length, jnp.sin(angles) / length)
    return (jnp.cos(angles), -jnp.sin(angles))


def apply_along(pencil, tables, axis_pos):
    real_table, imag_table = tables
    einsum_form = EINSUM_FORMS[axis_pos]
    real_in = pencil[0]
    imag_in = pencil[1]

    def product(matrix, values_in):
        return jnp.einsum(einsum_form, matrix, values_in, precision=lax.Precision.HIGHEST)

    real_out = product(real_table, real_in) - product(imag_table, imag_in)
    imag_out = product(real_table, imag_in) + product(imag_table, real_in)
    return jnp.stack([real_out, imag_out])


def scale_along(pencil, factors, axis_pos):
    layout = [1, 1, 1]
    layout[axis_pos] = -1
    real_scale = factors[0].reshape(layout)
    imag_scale = factors[1].reshape(layout)
    real_in = pencil[0]
    imag_in = pencil[1]
    return jnp.stack(
        [real_in * real_scale - imag_in * imag_scale, real_in * imag_scale + imag_in * real_scale]
    )


def advance_sweep(patches, lower_ghost, upper_ghost, matrix):
    slot_total = patches.shape[0]
    extended = jnp.concatenate([lower_ghost, patches, upper_ghost], axis=2)
    flattened = extended.reshape(slot_total, 48, -1)
    updated = jnp.einsum("kj,gjn->gkn", matrix, flattened, precision=lax.Precision.HIGHEST)
    updated = updated.reshape(slot_total, 2, 16, 16, 16)
    return jnp.transpose(updated, (0, 1, 3, 4, 2)).reshape(slot_total, 2, 16, 256)


def shards(base, fine_psi, counts, neighbors, base_cell):
    wide_count = lax.axis_size("wide")
    narrow_count = lax.axis_size("narrow")
    wide_index = lax.axis_index("wide")
    narrow_index = lax.axis_index("narrow")
    length = base.shape[3]
    rotation = rotation_angles(length)
    turning = (jnp.cos(rotation), -jnp.sin(rotation))
    forward = dft_tables(length, False)
    backward = dft_tables(length, True)
    working = scale_along(apply_along(base, forward, 2), turning, 2)
    working = scale_along(
        apply_along(
            lax.all_to_all(working, "narrow", split_axis=3, concat_axis=2, tiled=True), forward, 1
        ),
        turning,
        1,
    )
    working = apply_along(
        scale_along(
            apply_along(
                lax.all_to_all(working, "wide", split_axis=2, concat_axis=1, tiled=True), forward, 0
            ),
            turning,
            0,
        ),
        backward,
        0,
    )
    working = apply_along(
        lax.all_to_all(working, "wide", split_axis=1, concat_axis=2, tiled=True), backward, 1
    )
    drifted = apply_along(
        lax.all_to_all(working, "narrow", split_axis=2, concat_axis=3, tiled=True), backward, 2
    )
    rows_here = base.shape[1]
    cols_here = base.shape[2]
    slot_count = fine_psi.shape[0]
    slot_total = base_cell.shape[0]
    local_first = base_cell[:, :, 0] - wide_index * rows_here
    local_second = base_cell[:, :, 1] - narrow_index * cols_here
    mine = (
        (local_first >= 0)
        & (local_first < rows_here)
        & (local_second >= 0)
        & (local_second < cols_here)
    )
    clipped_first = jnp.clip(local_first, 0, rows_here - 1)
    clipped_second = jnp.clip(local_second, 0, cols_here - 1)
    flat_index = (clipped_first * cols_here + clipped_second) * length + base_cell[:, :, 2]
    picked = jnp.take(drifted.reshape(2, -1), flat_index.reshape(-1), axis=1)
    picked = jnp.where(mine.reshape(1, -1), picked, jnp.zeros_like(picked))
    terms = jnp.transpose(picked.reshape(2, slot_total, 6), (1, 0, 2)).reshape(slot_total, 12)
    edge_rows = lax.psum_scatter(terms, ("wide", "narrow"), scatter_dimension=0, tiled=True)
    devices_all = wide_count * narrow_count
    my_device = wide_index * narrow_count + narrow_index
    matrix = taylor_matrix()

    def pool_position(neighbor_ids):
        owner_device = jnp.maximum(neighbor_ids, 0) // slot_count
        relative = (owner_device - my_device + devices_all) % devices_all
        block_start = jnp.where(
            relative == 0, slot_count, jnp.where(relative == 1, 2 * slot_count, 0)
        )
        return block_start + jnp.maximum(neighbor_ids, 0) - owner_device * slot_count

    def ghost_layers(candidates, neighbor_ids, face_index):
        taken = jnp.take(candidates, pool_position(neighbor_ids), axis=0)
        edge_pairs = jnp.stack([edge_rows[:, face_index], edge_rows[:, 6 + face_index]], axis=1)
        constant = jnp.broadcast_to(edge_pairs[:, :, None, None], taken.shape)
        return jnp.where((neighbor_ids >= 0)[:, None, None, None], taken, constant)

    patches = fine_psi
    for subcycle in range(SUBCYCLES):
        for sweep_dim in range(3):
            face_slabs = jnp.stack([patches[:, :, :4, :], patches[:, :, 12:, :]], axis=1)
            from_lower = shifted(face_slabs, ("wide", "narrow"), 1)
            from_upper = shifted(face_slabs, ("wide", "narrow"), -1)
            candidates = jnp.concatenate([from_lower, face_slabs, from_upper], axis=0)
            lower_ghost = ghost_layers(candidates[:, 1], neighbors[:, 2 * sweep_dim], 2 * sweep_dim)
            upper_ghost = ghost_layers(
                candidates[:, 0], neighbors[:, 2 * sweep_dim + 1], 2 * sweep_dim + 1
            )
            patches = advance_sweep(patches, lower_ghost, upper_ghost, matrix)
    live = jnp.arange(slot_count, dtype=jnp.int32) < counts[0]
    fine_out = jnp.where(live[:, None, None, None], patches, jnp.zeros_like(patches))
    return (drifted, fine_out)


def solution(mesh):
    in_specs = (
        P(None, "wide", "narrow", None),
        P(("wide", "narrow"), None, None, None),
        P(("wide", "narrow")),
        P(("wide", "narrow"), None),
        P(),
    )
    out_specs = (P(None, "wide", "narrow", None), P(("wide", "narrow"), None, None, None))
    return jax.shard_map(shards, mesh=mesh, in_specs=in_specs, out_specs=out_specs, check_vma=False)
```

profile of v0, /device:TPU:32, one launch (start us, length us, event | category | flops | bytes accessed | tf_op | source)
XLA Modules:
  0.0 533.4 jit_solution(17543461520162834855)
XLA Ops:
  8.1 4.3 collective-permute-start
  12.4 10.1 %collective-permute-start.1 = (f32[4,2,2,4,256]{4,3,2,0,1:T(4,128)S(1)}, f32[4,2,2,4,256]{4,3,2,0,1:T(4,128)S(1)}, u32[]{:S(2)}, u32[]{:S(2)}) collective-permute-start(f32[4,2,2,4,256]{4,3,2,0,1:T(4,128)S(1)} %pad_maximum_fusion.18), channel_id=1, source_target_pairs={{1,0},{2,1},{3,2},{4,3},{5,4},{6,5},{7,6},{8,7},{9,8},{10,9},{11,1... | collective-permute-start | bytes 196616 | tf_op jit(solution)/shard_map/ppermute | solution.py:17
  22.5 2.0 fusion.24
  28.5 2.0 subtract_bitcast_fusion.2
  32.5 4.0 all-to-all-start
  40.0 5.3 all-to-all-done
  54.4 10.3 %all-to-all-start.1 = ((f32[64,1,432]{2,1,0:T(1,128)}), f32[64,1,432]{2,1,0:T(1,128)S(1)}, u32[]{:S(2)}, u32[]{:S(2)}) async-start(f32[64,1,432]{2,1,0:T(1,128)} %reshape.547), calls=%async_computation.1 | async-start | bytes 262144 | tf_op jit(solution)/shard_map/all_to_all | solution.py:110
  64.8 6.4 %all-to-all-done.1 = f32[64,1,432]{2,1,0:T(1,128)S(1)} async-done(((f32[64,1,432]{2,1,0:T(1,128)}), f32[64,1,432]{2,1,0:T(1,128)S(1)}, u32[]{:S(2)}, u32[]{:S(2)}) %all-to-all-start.1) | async-done | bytes 110624 | tf_op jit(solution)/shard_map/all_to_all | solution.py:110
  85.0 9.3 %all-to-all-start.2 = ((f32[64,1,432]{2,1,0:T(1,128)}), f32[64,1,432]{2,1,0:T(1,128)S(1)}, u32[]{:S(2)}, u32[]{:S(2)}) async-start(f32[64,1,432]{2,1,0:T(1,128)} %reshape.549), calls=%async_computation.2 | async-start | bytes 262144 | tf_op jit(solution)/shard_map/all_to_all | solution.py:119
  94.5 6.3 %all-to-all-done.2 = f32[64,1,432]{2,1,0:T(1,128)S(1)} async-done(((f32[64,1,432]{2,1,0:T(1,128)}), f32[64,1,432]{2,1,0:T(1,128)S(1)}, u32[]{:S(2)}, u32[]{:S(2)}) %all-to-all-start.2) | async-done | bytes 110624 | tf_op jit(solution)/shard_map/all_to_all | solution.py:119
  109.9 3.4 all-to-all-start.3
  113.8 8.4 %all-to-all-done.3 = f32[8,1,3456]{2,1,0:T(1,128)S(1)} async-done(((f32[8,1,3456]{2,1,0:T(1,128)}), f32[8,1,3456]{2,1,0:T(1,128)S(1)}, u32[]{:S(2)}, u32[]{:S(2)}) %all-to-all-start.3) | async-done | bytes 110624 | tf_op jit(solution)/shard_map/all_to_all | solution.py:122
  129.2 4.3 copy.126
  133.5 44.3 %gather_fusion = f32[12288,2]{1,0:T(8,128)} fusion(f32[2,13824]{0,1:T(8,128)} %copy.126, s32[12288]{0:T(1024)S(1)} %broadcast_clamp_fusion), kind=kCustom, calls=%fused_computation.12 | custom fusion | bytes 245760 | tf_op jit(solution)/shard_map/jit(_take)/gather | solution.py:139
  177.8 4.4 copy.127
  182.2 2.2 gather.10
  186.0 2.2 copy.128
  190.2 253.0 %all-reduce.3.cloned.1.call-done = f32[2048,12]{0,1:T(8,128)} async-done(((f32[2048,12]{0,1:T(8,128)}), f32[2048,12]{0,1:T(8,128)}) %all-reduce.3.cloned.1.call-update) | async-done | bytes 98320
  446.2 2.6 collective-permute-start.2
  448.8 8.4 %collective-permute-start.3 = (f32[4,2,2,4,256]{4,3,2,0,1:T(4,128)S(1)}, f32[4,2,2,4,256]{4,3,2,0,1:T(4,128)S(1)}, u32[]{:S(2)}, u32[]{:S(2)}) collective-permute-start(f32[4,2,2,4,256]{4,3,2,0,1:T(4,128)S(1)} %pad_maximum_fusion.19), channel_id=1, source_target_pairs={{1,0},{2,1},{3,2},{4,3},{5,4},{6,5},{7,6},{8,7},{9,8},{10,9},{11,1... | collective-permute-start | bytes 196616 | tf_op jit(solution)/shard_map/ppermute | solution.py:17
  464.0 9.3 %collective-permute-start.5 = (f32[4,2,2,4,256]{4,3,2,0,1:T(4,128)S(1)}, f32[4,2,2,4,256]{4,3,2,0,1:T(4,128)S(1)}, u32[]{:S(2)}, u32[]{:S(2)}) collective-permute-start(f32[4,2,2,4,256]{4,3,2,0,1:T(4,128)S(1)} %pad_maximum_fusion.20), channel_id=1, source_target_pairs={{1,0},{2,1},{3,2},{4,3},{5,4},{6,5},{7,6},{8,7},{9,8},{10,9},{11,1... | collective-permute-start | bytes 196616 | tf_op jit(solution)/shard_map/ppermute | solution.py:17
  479.9 9.1 %collective-permute-start.7 = (f32[4,2,2,4,256]{4,3,2,0,1:T(4,128)S(1)}, f32[4,2,2,4,256]{4,3,2,0,1:T(4,128)S(1)}, u32[]{:S(2)}, u32[]{:S(2)}) collective-permute-start(f32[4,2,2,4,256]{4,3,2,0,1:T(4,128)S(1)} %pad_maximum_fusion.21), channel_id=1, source_target_pairs={{1,0},{2,1},{3,2},{4,3},{5,4},{6,5},{7,6},{8,7},{9,8},{10,9},{11,1... | collective-permute-start | bytes 196616 | tf_op jit(solution)/shard_map/ppermute | solution.py:17
  495.8 9.1 %collective-permute-start.9 = (f32[4,2,2,4,256]{4,3,2,0,1:T(4,128)S(1)}, f32[4,2,2,4,256]{4,3,2,0,1:T(4,128)S(1)}, u32[]{:S(2)}, u32[]{:S(2)}) collective-permute-start(f32[4,2,2,4,256]{4,3,2,0,1:T(4,128)S(1)} %pad_maximum_fusion.22), channel_id=1, source_target_pairs={{1,0},{2,1},{3,2},{4,3},{5,4},{6,5},{7,6},{8,7},{9,8},{10,9},{11,1... | collective-permute-start | bytes 196616 | tf_op jit(solution)/shard_map/ppermute | solution.py:17
  511.7 9.1 %collective-permute-start.11 = (f32[4,2,2,4,256]{4,3,2,0,1:T(4,128)S(1)}, f32[4,2,2,4,256]{4,3,2,0,1:T(4,128)S(1)}, u32[]{:S(2)}, u32[]{:S(2)}) collective-permute-start(f32[4,2,2,4,256]{4,3,2,0,1:T(4,128)S(1)} %pad_maximum_fusion.23), channel_id=1, source_target_pairs={{1,0},{2,1},{3,2},{4,3},{5,4},{6,5},{7,6},{8,7},{9,8},{10,9},{11,1... | collective-permute-start | bytes 196616 | tf_op jit(solution)/shard_map/ppermute | solution.py:17
  (217 shorter events, 87.5 us)
Async XLA Ops:
  8.1 105.6 %collective-permute-start = (f32[4,2,2,4,256]{4,3,2,0,1:T(4,128)S(1)}, f32[4,2,2,4,256]{4,3,2,0,1:T(4,128)S(1)}, u32[]{:S(2)}, u32[]{:S(2)}) collective-permute-start(f32[4,2,2,4,256]{4,3,2,0,1:T(4,128)S(1)} %pad_maximum_fusion.18), channel_id=1, source_target_pairs={{511,0},{0,1},{1,2},{2,3},{3,4},{4,5},{5,6},{6,7},{7,8},{8,9},{9,1... | collective-permute-start | bytes 196616 | tf_op jit(solution)/shard_map/ppermute | solution.py:17
  12.4 101.3 %collective-permute-start.1 = (f32[4,2,2,4,256]{4,3,2,0,1:T(4,128)S(1)}, f32[4,2,2,4,256]{4,3,2,0,1:T(4,128)S(1)}, u32[]{:S(2)}, u32[]{:S(2)}) collective-permute-start(f32[4,2,2,4,256]{4,3,2,0,1:T(4,128)S(1)} %pad_maximum_fusion.18), channel_id=1, source_target_pairs={{1,0},{2,1},{3,2},{4,3},{5,4},{6,5},{7,6},{8,7},{9,8},{10,9},{11,1... | collective-permute-start | bytes 196616 | tf_op jit(solution)/shard_map/ppermute | solution.py:17
  22.5 14.5 %copy-start.2 = (s32[2048,6,3]{0,2,1:T(4,128)S(1)}, s32[2048,6,3]{0,2,1:T(4,128)}, u32[]{:S(2)}) copy-start(s32[2048,6,3]{0,2,1:T(4,128)} %param.11) | copy-start | bytes 442372
  32.5 7.0 %copy-start.1 = (s32[4,6]{1,0:T(4,128)S(1)}, s32[4,6]{1,0:T(4,128)}, u32[]{:S(2)}) copy-start(s32[4,6]{1,0:T(4,128)} %param.10) | copy-start | bytes 292
  32.5 12.8 %all-to-all-start = ((f32[8,1,3456]{2,1,0:T(1,128)}), f32[8,1,3456]{2,1,0:T(1,128)S(1)}, u32[]{:S(2)}, u32[]{:S(2)}) async-start(f32[8,1,3456]{2,1,0:T(1,128)} %reshape.545), calls=%async_computation | async-start | bytes 221184 | tf_op jit(solution)/shard_map/all_to_all | solution.py:102
  54.4 16.8 %all-to-all-start.1 = ((f32[64,1,432]{2,1,0:T(1,128)}), f32[64,1,432]{2,1,0:T(1,128)S(1)}, u32[]{:S(2)}, u32[]{:S(2)}) async-start(f32[64,1,432]{2,1,0:T(1,128)} %reshape.547), calls=%async_computation.1 | async-start | bytes 262144 | tf_op jit(solution)/shard_map/all_to_all | solution.py:110
  85.0 15.8 %all-to-all-start.2 = ((f32[64,1,432]{2,1,0:T(1,128)}), f32[64,1,432]{2,1,0:T(1,128)S(1)}, u32[]{:S(2)}, u32[]{:S(2)}) async-start(f32[64,1,432]{2,1,0:T(1,128)} %reshape.549), calls=%async_computation.2 | async-start | bytes 262144 | tf_op jit(solution)/shard_map/all_to_all | solution.py:119
  109.9 12.3 %all-to-all-start.3 = ((f32[8,1,3456]{2,1,0:T(1,128)}), f32[8,1,3456]{2,1,0:T(1,128)S(1)}, u32[]{:S(2)}, u32[]{:S(2)}) async-start(f32[8,1,3456]{2,1,0:T(1,128)} %reshape.551), calls=%async_computation.3 | async-start | bytes 221184 | tf_op jit(solution)/shard_map/all_to_all | solution.py:122
  113.2 330.0 %all-reduce.3.cloned.1.call-start = ((), (), s32[]{:S(2)}) async-start(), calls=%async_computation.4 | async-start | bytes 262144
  186.0 258.6 %copy-start = (f32[4,2,16,256]{3,2,1,0:T(8,128)S(1)}, f32[4,2,16,256]{3,2,1,0:T(8,128)}, u32[]{:S(2)}) copy-start(f32[4,2,16,256]{3,2,1,0:T(8,128)} %param.8) | copy-start | bytes 393220
  446.2 11.3 %collective-permute-start.2 = (f32[4,2,2,4,256]{4,3,2,0,1:T(4,128)S(1)}, f32[4,2,2,4,256]{4,3,2,0,1:T(4,128)S(1)}, u32[]{:S(2)}, u32[]{:S(2)}) collective-permute-start(f32[4,2,2,4,256]{4,3,2,0,1:T(4,128)S(1)} %pad_maximum_fusion.19), channel_id=1, source_target_pairs={{511,0},{0,1},{1,2},{2,3},{3,4},{4,5},{5,6},{6,7},{7,8},{8,9},{9,1... | collective-permute-start | bytes 196616 | tf_op jit(solution)/shard_map/ppermute | solution.py:17
  448.8 10.3 %collective-permute-start.3 = (f32[4,2,2,4,256]{4,3,2,0,1:T(4,128)S(1)}, f32[4,2,2,4,256]{4,3,2,0,1:T(4,128)S(1)}, u32[]{:S(2)}, u32[]{:S(2)}) collective-permute-start(f32[4,2,2,4,256]{4,3,2,0,1:T(4,128)S(1)} %pad_maximum_fusion.19), channel_id=1, source_target_pairs={{1,0},{2,1},{3,2},{4,3},{5,4},{6,5},{7,6},{8,7},{9,8},{10,9},{11,1... | collective-permute-start | bytes 196616 | tf_op jit(solution)/shard_map/ppermute | solution.py:17
  462.1 11.3 %collective-permute-start.4 = (f32[4,2,2,4,256]{4,3,2,0,1:T(4,128)S(1)}, f32[4,2,2,4,256]{4,3,2,0,1:T(4,128)S(1)}, u32[]{:S(2)}, u32[]{:S(2)}) collective-permute-start(f32[4,2,2,4,256]{4,3,2,0,1:T(4,128)S(1)} %pad_maximum_fusion.20), channel_id=1, source_target_pairs={{511,0},{0,1},{1,2},{2,3},{3,4},{4,5},{5,6},{6,7},{7,8},{8,9},{9,1... | collective-permute-start | bytes 196616 | tf_op jit(solution)/shard_map/ppermute | solution.py:17
  464.0 11.0 %collective-permute-start.5 = (f32[4,2,2,4,256]{4,3,2,0,1:T(4,128)S(1)}, f32[4,2,2,4,256]{4,3,2,0,1:T(4,128)S(1)}, u32[]{:S(2)}, u32[]{:S(2)}) collective-permute-start(f32[4,2,2,4,256]{4,3,2,0,1:T(4,128)S(1)} %pad_maximum_fusion.20), channel_id=1, source_target_pairs={{1,0},{2,1},{3,2},{4,3},{5,4},{6,5},{7,6},{8,7},{9,8},{10,9},{11,1... | collective-permute-start | bytes 196616 | tf_op jit(solution)/shard_map/ppermute | solution.py:17
  478.0 11.7 %collective-permute-start.6 = (f32[4,2,2,4,256]{4,3,2,0,1:T(4,128)S(1)}, f32[4,2,2,4,256]{4,3,2,0,1:T(4,128)S(1)}, u32[]{:S(2)}, u32[]{:S(2)}) collective-permute-start(f32[4,2,2,4,256]{4,3,2,0,1:T(4,128)S(1)} %pad_maximum_fusion.21), channel_id=1, source_target_pairs={{511,0},{0,1},{1,2},{2,3},{3,4},{4,5},{5,6},{6,7},{7,8},{8,9},{9,1... | collective-permute-start | bytes 196616 | tf_op jit(solution)/shard_map/ppermute | solution.py:17
  479.9 11.0 %collective-permute-start.7 = (f32[4,2,2,4,256]{4,3,2,0,1:T(4,128)S(1)}, f32[4,2,2,4,256]{4,3,2,0,1:T(4,128)S(1)}, u32[]{:S(2)}, u32[]{:S(2)}) collective-permute-start(f32[4,2,2,4,256]{4,3,2,0,1:T(4,128)S(1)} %pad_maximum_fusion.21), channel_id=1, source_target_pairs={{1,0},{2,1},{3,2},{4,3},{5,4},{6,5},{7,6},{8,7},{9,8},{10,9},{11,1... | collective-permute-start | bytes 196616 | tf_op jit(solution)/shard_map/ppermute | solution.py:17
  493.9 11.1 %collective-permute-start.8 = (f32[4,2,2,4,256]{4,3,2,0,1:T(4,128)S(1)}, f32[4,2,2,4,256]{4,3,2,0,1:T(4,128)S(1)}, u32[]{:S(2)}, u32[]{:S(2)}) collective-permute-start(f32[4,2,2,4,256]{4,3,2,0,1:T(4,128)S(1)} %pad_maximum_fusion.22), channel_id=1, source_target_pairs={{511,0},{0,1},{1,2},{2,3},{3,4},{4,5},{5,6},{6,7},{7,8},{8,9},{9,1... | collective-permute-start | bytes 196616 | tf_op jit(solution)/shard_map/ppermute | solution.py:17
  495.8 11.0 %collective-permute-start.9 = (f32[4,2,2,4,256]{4,3,2,0,1:T(4,128)S(1)}, f32[4,2,2,4,256]{4,3,2,0,1:T(4,128)S(1)}, u32[]{:S(2)}, u32[]{:S(2)}) collective-permute-start(f32[4,2,2,4,256]{4,3,2,0,1:T(4,128)S(1)} %pad_maximum_fusion.22), channel_id=1, source_target_pairs={{1,0},{2,1},{3,2},{4,3},{5,4},{6,5},{7,6},{8,7},{9,8},{10,9},{11,1... | collective-permute-start | bytes 196616 | tf_op jit(solution)/shard_map/ppermute | solution.py:17
  509.8 11.7 %collective-permute-start.10 = (f32[4,2,2,4,256]{4,3,2,0,1:T(4,128)S(1)}, f32[4,2,2,4,256]{4,3,2,0,1:T(4,128)S(1)}, u32[]{:S(2)}, u32[]{:S(2)}) collective-permute-start(f32[4,2,2,4,256]{4,3,2,0,1:T(4,128)S(1)} %pad_maximum_fusion.23), channel_id=1, source_target_pairs={{511,0},{0,1},{1,2},{2,3},{3,4},{4,5},{5,6},{6,7},{7,8},{8,9},{9,1... | collective-permute-start | bytes 196616 | tf_op jit(solution)/shard_map/ppermute | solution.py:17
  511.7 11.0 %collective-permute-start.11 = (f32[4,2,2,4,256]{4,3,2,0,1:T(4,128)S(1)}, f32[4,2,2,4,256]{4,3,2,0,1:T(4,128)S(1)}, u32[]{:S(2)}, u32[]{:S(2)}) collective-permute-start(f32[4,2,2,4,256]{4,3,2,0,1:T(4,128)S(1)} %pad_maximum_fusion.23), channel_id=1, source_target_pairs={{1,0},{2,1},{3,2},{4,3},{5,4},{6,5},{7,6},{8,7},{9,8},{10,9},{11,1... | collective-permute-start | bytes 196616 | tf_op jit(solution)/shard_map/ppermute | solution.py:17
Sparse Core Ops, SparseCore 0:
  189.1 254.0 all-reduce.2
where the time goes:
time: 539 us; the launch traced here: 533 us
  waiting for transfers between devices  287 us (53%)
  starting transfers between devices  97.1 us (18%)
  local copies, waits for them, and re-layouts  91.9 us (17%)
  matrix products  32 us (6%)
  between operations  16 us (3%)
  other arithmetic  9.54 us (2%)
    unnamed x2, waiting for transfers between devices  253 us
    ppermute x12, starting transfers between devices, shifted(): return lax.ppermute(block, axis, route)  69.7 us
    gather x3, local copies, waits for them, and re-layouts, shards(): picked = jnp.take(drifted.reshape(2, -1), flat_index.reshape(-1), axis=1)  50.9 us
    dot_general x16, matrix products, product(): jnp.einsum(einsum_form, matrix, values_in, precision=lax.Precision.HIGHEST)  21.2 us
  transfers between devices with their start and end apart: 17, of which 10 were waited for; matrix products, arithmetic and copies ran while one was open for 9% of the time, Pallas kernels for 0%

commit v1 on v0

v1 whole, which is shorter than its diff:
```python
import jax
import jax.numpy as jnp
import ml_dtypes
import numpy as np
from jax import lax
from jax.experimental import pallas as pl
from jax.experimental.pallas import tpu as pltpu
from jax.sharding import PartitionSpec as P

SUBCYCLES = 2
PHASE_RATE = 8.0
TAYLOR_STEP = 0.6
EDGE = 16
CELLS = EDGE * EDGE
LANES = 128
REACH = 6
VMEM = pl.BlockSpec(memory_space=pltpu.VMEM)
SMEM = pl.BlockSpec(memory_space=pltpu.SMEM)
PARAMS = pltpu.CompilerParams(vmem_limit_bytes=48 * 2**20)
F32 = jnp.float32
BF16 = jnp.bfloat16


def two_parts(matrix):
    high = matrix.astype(ml_dtypes.bfloat16)
    low = (matrix - high.astype(np.float64)).astype(ml_dtypes.bfloat16)
    return high, low


def circulant(length):
    signed = np.fft.fftfreq(length, 1.0 / length)
    phase = np.exp(-1j * PHASE_RATE * (2.0 * np.pi * signed / length) ** 2)
    kernel = np.fft.ifft(phase)
    index = np.arange(length)
    matrix = kernel[(index[:, None] - index[None, :]) % length]
    return matrix.real, matrix.imag


def taylor_parts():
    laplace = -2.0 * np.eye(24) + np.eye(24, k=1) + np.eye(24, k=-1)
    squared = laplace @ laplace
    c = TAYLOR_STEP
    real = np.eye(24) - c**2 / 2.0 * squared + c**4 / 24.0 * squared @ squared
    imag = c * laplace - c**3 / 6.0 * squared @ laplace
    parts = []
    for rows in (real[4:20], imag[4:20]):
        ghost = np.zeros((EDGE, EDGE))
        ghost[:, 12:] = rows[:, :4]
        ghost[:, :4] = rows[:, 20:]
        parts.append((rows[:, 4:20], ghost))
    return parts


def sweep_tables():
    (own_r, ghost_r), (own_i, ghost_i) = taylor_parts()
    left = np.concatenate(
        [
            np.block([[own_r, -own_i], [own_i, own_r]]),
            np.block([[ghost_r, -ghost_i], [ghost_i, ghost_r]]),
        ],
        1,
    )
    eye = np.eye(EDGE)

    def right(form):
        return np.block([[form(own_r), form(own_i)], [form(ghost_r), form(ghost_i)]])

    middle = right(lambda t: np.kron(t.T, eye))
    last = right(lambda t: np.kron(eye, t.T))
    high, low = two_parts(left)
    return np.concatenate([high, high, low], 1), *two_parts(middle), *two_parts(last)


def split(values):
    high = values.astype(BF16)
    return high, (values - high.astype(F32)).astype(BF16)


def mm(a, b):
    return jnp.dot(a, b, preferred_element_type=F32)


def mm3(a, b):
    return mm(a[0], b[0]) + (mm(a[1], b[0]) + mm(a[0], b[1]))


def along_last(rows_here, cols_here, parts, base_ref, rh, rl, ih, il, out_ref):
    plane = rows_here * cols_here
    x = split(base_ref[...])
    pr = mm3(x, (rh[...], rl[...]))
    pi = mm3(x, (ih[...], il[...]))
    done = (pr[:plane] - pi[plane:], pi[:plane] + pr[plane:])
    chunk = done[0].shape[1] // parts
    pad = jnp.zeros((cols_here, LANES - rows_here * chunk), F32)
    for n in range(parts):
        for p in range(2):
            pieces = [
                done[p][cols_here * x : cols_here * (x + 1), chunk * n : chunk * (n + 1)]
                for x in range(rows_here)
            ]
            row = (2 * n + p) * cols_here
            out_ref[row : row + cols_here, :] = jnp.concatenate(pieces + [pad], 1)


def along_second(rows_here, chunk, wide, x_ref, wh, wl, out_ref):
    done = mm3((wh[...], wl[...]), split(x_ref[...]))
    pad = jnp.zeros((wide, LANES - rows_here * chunk), F32)
    for p in range(2):
        for x in range(rows_here):
            pieces = [
                done[(p * rows_here + j) * wide : (p * rows_here + j + 1) * wide, chunk * x : chunk * (x + 1)]
                for j in range(rows_here)
            ]
            out_ref[pl.ds(p * rows_here + x, wide, stride=8), :] = jnp.concatenate(pieces + [pad], 1)
    blank = jnp.zeros((wide, LANES), F32)
    for r in range(2 * rows_here, 8):
        out_ref[pl.ds(r, wide, stride=8), :] = blank


def along_first(rows_here, chunk, wide, narrow, slots, place_ref, cell_ref, x_ref, wh, wl, out_ref, o_ref, v_ref):
    used = rows_here * chunk
    lines = rows_here * wide
    groups = cell_ref.shape[1]
    o_ref[...] = mm3((wh[...], wl[...]), split(x_ref[...]))
    turned = []
    for p in range(2):
        natural = [o_ref[pl.ds(p * rows_here + x, wide, stride=8), :] for x in range(rows_here)]
        natural.append(jnp.zeros((256 - lines, LANES), F32))
        turned.append(jnp.concatenate(natural, 0).T[:used])
    high, low = split(jnp.concatenate(turned, 0))
    left = jnp.concatenate([high, low], 0)
    second_start = place_ref[0] * rows_here
    last_start = place_ref[1] * chunk
    step = 256
    line_of = lax.broadcasted_iota(jnp.int32, (256, step), 0)
    lane_of = lax.broadcasted_iota(jnp.int32, (used, step), 0)

    def body(c, carry):
        at = pl.multiple_of(c * step, step)
        for f in range(6):
            first = cell_ref[f : f + 1, pl.ds(at, step)]
            second = cell_ref[6 + f : 7 + f, pl.ds(at, step)] - second_start
            last = cell_ref[12 + f : 13 + f, pl.ds(at, step)] - last_start
            mine = (second >= 0) & (second < rows_here) & (last >= 0) & (last < chunk)
            owner = first // rows_here
            line = (first - owner * rows_here) * wide + owner
            lane = jnp.where(mine, second * chunk + last, -1)
            hot = jnp.where(line_of == line, 1.0, 0.0).astype(BF16)
            taken = mm(left, hot)
            keep = lane_of == lane
            for p in range(2):
                both = taken[p * used : (p + 1) * used] + taken[(2 + p) * used : (3 + p) * used]
                v_ref[p * 8 + f : p * 8 + f + 1, pl.ds(at + LANES, step)] = jnp.sum(
                    jnp.where(keep, both, 0.0), axis=0, keepdims=True
                )
        return carry

    lax.fori_loop(0, groups // step, body, 0)
    v_ref[:, :LANES] = v_ref[:, groups : groups + LANES]
    v_ref[:, groups + LANES :] = v_ref[:, LANES : 2 * LANES]
    per_row = narrow * slots
    window = per_row + 10 * slots
    here = LANES - used
    for w in range(wide):
        start = LANES + w * per_row - 5 * slots
        zero = v_ref[0:8, start : start + window]
        one = v_ref[8:16, start : start + window]
        own = o_ref[8 * w : 8 * w + 8, :used]
        out_ref[16 * w : 16 * w + 8, :] = jnp.concatenate([own, one[:, :here]], 1)
        rest = jnp.zeros((8, LANES - window - (window - here)), F32)
        out_ref[16 * w + 8 : 16 * w + 16, :] = jnp.concatenate([zero, one[:, here:], rest], 1)


def forward_rows(wide, narrow, x_ref, out_ref):
    per = wide // narrow
    low = jnp.zeros((8, LANES), F32)
    top = jnp.zeros((8, LANES), F32)
    for w in range(wide):
        tile = x_ref[16 * w : 16 * w + 8, :]
        low += tile
        top += x_ref[16 * w + 8 : 16 * w + 16, :]
        row = (w // per) * (8 * per + 16) + 8 * (w % per)
        out_ref[row : row + 8, :] = tile
    for n in range(narrow):
        row = n * (8 * per + 16) + 8 * per
        out_ref[row : row + 8, :] = low
        out_ref[row + 8 : row + 16, :] = top


def unpack(rows_here, chunk, per, narrow, x_ref, out_ref, lo_ref, hi_ref):
    block = 8 * per + 16
    cols = per * rows_here
    length = out_ref.shape[1]
    for r in range(2 * rows_here):
        tiles = [x_ref[pl.ds(n * block + r, per, stride=8), :] for n in range(narrow)]
        for y in range(rows_here):
            pieces = [t[:, chunk * y : chunk * (y + 1)] for t in tiles]
            line = jnp.concatenate(pieces + [jnp.zeros((per, 2 * LANES - length), F32)], 1)
            lo_ref[pl.ds(r * cols + y, per, stride=rows_here), :] = line[:, :LANES]
            hi_ref[pl.ds(r * cols + y, per, stride=rows_here), :] = line[:, LANES:]
    out_ref[:, :LANES] = lo_ref[...]
    out_ref[:, LANES:] = hi_ref[:, : length - LANES]


def sweeps(
    slots, narrow, per, used, place_ref, count_ref, near_ref, recv_ref, before_ref, row_ref, after_ref,
    left_ref, mid_h, mid_l, last_h, last_l, out_ref, one_ref, two_ref, high_ref, low_ref, edge_ref, edge_smem, sem,
):
    block = 8 * per + 16
    window = narrow * slots + 10 * slots
    here = LANES - used
    low = jnp.zeros((8, LANES), F32)
    top = jnp.zeros((8, LANES), F32)
    for n in range(narrow):
        row = n * block + 8 * per
        low += recv_ref[row : row + 8, :]
        top += recv_ref[row + 8 : row + 16, :]
    edge_ref[0:8, :] = top
    edge_ref[8:16, :] = jnp.concatenate(
        [low[:, used:], top[:, window : 2 * window - here], jnp.zeros((8, LANES - window), F32)], 1
    )
    copy = pltpu.make_async_copy(edge_ref, edge_smem, sem)
    copy.start()
    mine = place_ref[1]
    total = 2 * REACH + 1
    for r in range(total):
        at = mine + r + narrow - REACH

        @pl.when(at < narrow)
        def _(r=r, at=at):
            one_ref[slots * r : slots * (r + 1)] = before_ref[at - (narrow - REACH), :, 0 : 2 * EDGE, :]

        @pl.when((at >= narrow) & (at < 2 * narrow))
        def _(r=r, at=at):
            one_ref[slots * r : slots * (r + 1)] = row_ref[at - narrow, :, 0 : 2 * EDGE, :]

        @pl.when(at >= 2 * narrow)
        def _(r=r, at=at):
            one_ref[slots * r : slots * (r + 1)] = after_ref[at - 2 * narrow, :, 0 : 2 * EDGE, :]

    copy.wait()
    rows = lax.broadcasted_iota(jnp.int32, (2 * EDGE, CELLS), 0)
    lanes = lax.broadcasted_iota(jnp.int32, (2 * EDGE, CELLS), 1)
    real = rows < EDGE
    upper_half = (rows % EDGE >= 8, lanes >= CELLS // 2, lanes % EDGE >= 8)
    tables = (None, (mid_h, mid_l), (last_h, last_l))
    held = [one_ref, two_ref]
    for s in range(3 * SUBCYCLES):
        k = s % 3
        source, target = held[s % 2], held[1 - s % 2]
        first, end = slots * (s + 1), slots * (total - s - 1)

        def ghost(q, face, source=source):
            near = near_ref[q * 6 + face]
            lane = q + slots * (mine - 1)
            flat = jnp.where(real, edge_smem[face, lane], edge_smem[8 + face, lane])
            return jnp.where(near >= 0, source[jnp.maximum(near, 0)], flat)

        def gather(q, k=k, source=source, ghost=ghost):
            return source[q], jnp.where(upper_half[k], ghost(q, 2 * k), ghost(q, 2 * k + 1))

        if k == 0:

            def step(q, carry, gather=gather, target=target):
                high, low_ = split(jnp.concatenate(gather(q), 0))
                target[q] = mm(left_ref[...], jnp.concatenate([high, low_, high], 0))
                return carry

            lax.fori_loop(first, end, step, 0, unroll=4)
        else:
            wh, wl = tables[k]

            def step(d, carry, gather=gather, target=target, wh=wh, wl=wl):
                for i in range(slots):
                    high, low_ = split(jnp.concatenate(gather(slots * d + i), 1))
                    high_ref[2 * EDGE * i : 2 * EDGE * (i + 1), :] = high
                    low_ref[2 * EDGE * i : 2 * EDGE * (i + 1), :] = low_
                done = mm3((high_ref[...], low_ref[...]), (wh[...], wl[...]))
                for i in range(slots):
                    a, b = 2 * EDGE * i, 2 * EDGE * i + EDGE
                    re, im = done[a:b], done[b : b + EDGE]
                    target[slots * d + i, 0:EDGE, :] = re[:, :CELLS] - im[:, CELLS:]
                    target[slots * d + i, EDGE:, :] = im[:, :CELLS] + re[:, CELLS:]
                return carry

            lax.fori_loop(first // slots, end // slots, step, 0)
    final = held[0]
    for i in range(slots):
        value = final[slots * REACH + i]
        out_ref[i] = jnp.where(i < count_ref[0], value, jnp.zeros_like(value))


def shifted(block, axis, distance):
    devices = range(lax.axis_size(axis))
    route = [((i - distance) % len(devices), i) for i in devices]
    return lax.ppermute(block, axis, route)


def call(kernel, out_rows, out_cols, specs, scratch=()):
    return pl.pallas_call(
        kernel,
        out_shape=jax.ShapeDtypeStruct((out_rows, out_cols), F32),
        in_specs=specs,
        out_specs=VMEM,
        scratch_shapes=list(scratch),
        compiler_params=PARAMS,
    )


def exchange(block, axis):
    parts = lax.axis_size(axis)
    shape = (parts, block.shape[0] // parts, block.shape[1])
    return lax.all_to_all(block.reshape(shape), axis, split_axis=0, concat_axis=0, tiled=True).reshape(block.shape)


def shards(base, fine_psi, counts, neighbors, base_cell):
    wide = lax.axis_size("wide")
    narrow = lax.axis_size("narrow")
    w_at = lax.axis_index("wide")
    n_at = lax.axis_index("narrow")
    _, rows_here, cols_here, length = base.shape
    slots = fine_psi.shape[0]
    chunk = length // narrow
    per = wide // narrow
    used = rows_here * chunk
    place = jnp.stack([w_at, n_at]).astype(jnp.int32)

    numbers = jnp.pad(neighbors.astype(F32)[:, None, :], ((0, 0), (0, 7), (0, CELLS - 6)))
    packet = jnp.concatenate([fine_psi.reshape(slots, 2 * EDGE, CELLS), numbers], 1)
    row = lax.all_gather(packet, "narrow", axis=0, tiled=False)
    before = shifted(row[narrow - REACH :], "wide", 1)
    after = shifted(row[:REACH], "wide", -1)

    kr, ki = circulant(length)
    first_axis = [jnp.asarray(t) for m in (kr, ki) for t in two_parts(m)]
    sent = call(
        lambda *refs: along_last(rows_here, cols_here, narrow, *refs), narrow * 2 * cols_here, LANES, [VMEM] * 5
    )(base.reshape(2 * rows_here * cols_here, length), *first_axis)
    got = exchange(sent, "narrow")

    full = np.stack([np.stack([kr, -ki]), np.stack([ki, kr])])
    second = full.reshape(2, 2, wide, rows_here, narrow, cols_here).transpose(0, 3, 2, 4, 1, 5)
    second = second.reshape(2 * length, 2 * length)
    sent = call(lambda *refs: along_second(rows_here, chunk, wide, *refs), wide * 8, LANES, [VMEM] * 3)(
        got, *[jnp.asarray(t) for t in two_parts(second)]
    )
    got = exchange(sent, "wide")

    third = np.zeros((wide, 8, wide, 8))
    blocks = full.reshape(2, 2, wide, rows_here, wide, rows_here).transpose(2, 0, 3, 4, 1, 5)
    third[:, : 2 * rows_here, :, : 2 * rows_here] = blocks.reshape(wide, 2 * rows_here, wide, 2 * rows_here)
    third = third.reshape(wide * 8, wide * 8)
    cells = jnp.transpose(base_cell, (2, 1, 0)).reshape(18, base_cell.shape[0])
    sent = call(
        lambda *refs: along_first(rows_here, chunk, wide, narrow, slots, *refs),
        wide * 16,
        LANES,
        [SMEM] + [VMEM] * 4,
        [pltpu.VMEM((wide * 8, LANES), F32), pltpu.VMEM((16, base_cell.shape[0] + 2 * LANES), F32)],
    )(place, cells, got, *[jnp.asarray(t) for t in two_parts(third)])
    got = exchange(sent, "wide")
    sent = call(lambda *refs: forward_rows(wide, narrow, *refs), narrow * (8 * per + 16), LANES, [VMEM])(got)
    got = exchange(sent, "narrow")
    drifted = call(
        lambda *refs: unpack(rows_here, chunk, per, narrow, *refs), 2 * rows_here * cols_here, length, [VMEM],
        [pltpu.VMEM((2 * rows_here * cols_here, LANES), F32)] * 2,
    )(got)

    devices = wide * narrow
    mine = w_at * narrow + n_at
    numbers = jnp.concatenate([before[:, :, 2 * EDGE, :6], row[:, :, 2 * EDGE, :6], after[:, :, 2 * EDGE, :6]], 0)
    total = 2 * REACH + 1
    numbers = lax.dynamic_slice_in_dim(numbers, n_at, total, 0).astype(jnp.int32)
    owner = numbers // slots
    relative = (owner - mine + REACH + devices) % devices
    near = jnp.where(numbers >= 0, relative * slots + numbers - owner * slots, -1)
    near = jnp.where(near < total * slots, near, -1).reshape(-1)
    tables = [jnp.asarray(t) for t in sweep_tables()]
    fine = pl.pallas_call(
        lambda *refs: sweeps(slots, narrow, per, used, *refs),
        out_shape=jax.ShapeDtypeStruct((slots, 2 * EDGE, CELLS), F32),
        in_specs=[SMEM] * 3 + [VMEM] * 9,
        out_specs=VMEM,
        scratch_shapes=[
            pltpu.VMEM((total * slots, 2 * EDGE, CELLS), F32),
            pltpu.VMEM((total * slots, 2 * EDGE, CELLS), F32),
            pltpu.VMEM((slots * 2 * EDGE, 2 * CELLS), BF16),
            pltpu.VMEM((slots * 2 * EDGE, 2 * CELLS), BF16),
            pltpu.VMEM((16, LANES), F32),
            pltpu.SMEM((16, LANES), F32),
            pltpu.SemaphoreType.DMA,
        ],
        compiler_params=PARAMS,
    )(place, counts, near, got, before, row, after, *tables)
    return (drifted.reshape(base.shape), fine.reshape(fine_psi.shape))


def solution(mesh):
    in_specs = (
        P(None, "wide", "narrow", None),
        P(("wide", "narrow"), None, None, None),
        P(("wide", "narrow")),
        P(("wide", "narrow"), None),
        P(),
    )
    out_specs = (P(None, "wide", "narrow", None), P(("wide", "narrow"), None, None, None))
    return jax.shard_map(shards, mesh=mesh, in_specs=in_specs, out_specs=out_specs, check_vma=False)
```

time: 539 us -> 135 us (0.25)
  the two profiles are of different devices: /device:TPU:32 before, /device:TPU:1 now
where the time goes in v1:
time: 135 us; the launch traced here: 134 us
  waiting for transfers between devices  35.8 us (27%)
  starting transfers between devices  26.3 us (19%)
  Pallas kernels  22.6 us (17%)
  blocking collectives  19.6 us (15%)
  between operations  14.9 us (11%)
  local copies, waits for them, and re-layouts  12.2 us (9%)
  other arithmetic  2.52 us (2%)
    all_to_all x3, waiting for transfers between devices, exchange(): lax.all_to_all(block.reshape(shape), axis, split_axis=0, concat_axis=0, t...  35.8 us
    all_to_all x3, starting transfers between devices, exchange(): lax.all_to_all(block.reshape(shape), axis, split_axis=0, concat_axis=0, t...  20.7 us
    all_to_all x1, blocking collectives, exchange(): lax.all_to_all(block.reshape(shape), axis, split_axis=0, concat_axis=0, t...  19.6 us
    pallas_call x1, Pallas kernels, shards(): pl.pallas_call(lambda *refs: sweeps(slots, narrow, per, used, *refs), out...  13.3 us
    unnamed x32, local copies, waits for them, and re-layouts  7.64 us
    pallas_call x1, Pallas kernels, shards(): call(lambda *refs: along_first(rows_here, chunk, wide, narrow, slots, *re...  5.91 us
    ppermute x2, starting transfers between devices, shifted(): return lax.ppermute(block, axis, route)  5.59 us
    slice x1, local copies, waits for them, and re-layouts, shards(): before = shifted(row[narrow - REACH:], 'wide', 1)  2.91 us
  transfers between devices with their start and end apart: 6, of which 3 were waited for; matrix products, arithmetic and copies ran while one was open for 2% of the time, Pallas kernels for 7%

profile of v1, /device:TPU:1, one launch (start us, length us, event | category | flops | bytes accessed | tf_op | source)
XLA Modules:
  0.0 134.0 jit_solution(10251243189823296759)
XLA Ops:
  8.0 1.6 %select_maximum_fusion = f32[4,40,256]{2,1,0:T(8,128)} fusion(f32[4,1,6]{2,1,0:T(1,128)S(1)} %bitcast.40, f32[4,32,256]{2,1,0:T(8,128)} %bitcast.36), kind=kLoop, calls=%fused_computation | loop fusion | flops 122880 | bytes 295008 | tf_op jit(solution)/shard_map/concatenate | solution.py:329
  9.6 0.9 copy-done.9
  10.5 0.9 copy-done.10
  11.4 0.9 copy-done.11
  12.3 0.9 copy-done.12
  13.2 0.9 copy-done.13
  14.6 19.6 %all_to_all.20 = f32[8,48,128]{2,1,0:T(8,128)S(1)} all-to-all(f32[8,48,128]{2,1,0:T(8,128)S(1)} %bitcast.31), channel_id=1, replica_groups=mesh['wide'=64,'narrow'=8] {'narrow'}, dimensions={0} | all-to-all | bytes 393216 | tf_op jit(solution)/shard_map/all_to_all | solution.py:313
  34.2 1.2 shard_map.186
  35.4 12.6 %all-to-all-start.1 = ((f32[64,8,128]{2,1,0:T(8,128)}), f32[64,8,128]{2,1,0:T(8,128)S(1)}, u32[]{:S(2)}, u32[]{:S(2)}) async-start(f32[64,8,128]{2,1,0:T(8,128)} %bitcast.6), calls=%async_computation.1 | async-start | bytes 524288 | tf_op jit(solution)/shard_map/all_to_all | solution.py:313
  48.2 12.9 %all-to-all-done.1 = f32[64,8,128]{2,1,0:T(8,128)S(1)} async-done(((f32[64,8,128]{2,1,0:T(8,128)}), f32[64,8,128]{2,1,0:T(8,128)S(1)}, u32[]{:S(2)}, u32[]{:S(2)}) %all-to-all-start.1) | async-done | bytes 262176 | tf_op jit(solution)/shard_map/all_to_all | solution.py:313
  61.2 5.9 %shard_map.187 = f32[1024,128]{1,0:T(8,128)} custom-call(s32[2]{0:T(128)S(1)} %pad_add_fusion.refs_0_, s32[18,2048]{1,0:T(8,128)S(1)} %reshape.46.refs_1_, f32[512,128]{1,0:T(8,128)S(1)} %bitcast.29, bf16[512,512]{1,0:T(8,128)(2,1)S(1)} %copy-done.5, bf16[512,512]{1,0:T(8,128)(2,1)S(1)} %copy-done.6), custom_call_target="tpu_custom_call" | custom-call | tf_op jit(solution)/shard_map/pallas_call | solution.py:354
  67.1 4.7 %all-to-all-start.2 = ((f32[64,16,128]{2,1,0:T(8,128)}), f32[64,16,128]{2,1,0:T(8,128)S(1)}, u32[]{:S(2)}, u32[]{:S(2)}) async-start(f32[64,16,128]{2,1,0:T(8,128)} %bitcast.8), calls=%async_computation.2 | async-start | bytes 1048576 | tf_op jit(solution)/shard_map/all_to_all | solution.py:313
  71.8 2.9 %fusion.8 = (f32[24,40,256]{2,1,0:T(8,128)}, f32[24,40,256]{2,1,0:T(8,128)}) fusion(f32[32,40,256]{2,1,0:T(8,128)} %all-gather.3.cloned.1.call-done), kind=kLoop, calls=%fused_computation.22 | loop fusion | bytes 3932160 | tf_op jit(solution)/shard_map/slice | solution.py:331
  74.7 3.7 %collective-permute-start = (f32[6,4,40,256]{3,2,1,0:T(8,128)}, f32[6,4,40,256]{3,2,1,0:T(8,128)S(1)}, u32[]{:S(2)}, u32[]{:S(2)}) collective-permute-start(f32[6,4,40,256]{3,2,1,0:T(8,128)} %bitcast.15), channel_id=1, source_target_pairs={{504,0},{0,8},{8,16},{16,24},{24,32},{32,40},{40,48},{48,56},{56,6... | collective-permute-start | bytes 2949128 | tf_op jit(solution)/shard_map/ppermute | solution.py:296
  78.4 1.9 %collective-permute-start.1 = (f32[6,4,40,256]{3,2,1,0:T(8,128)}, f32[6,4,40,256]{3,2,1,0:T(8,128)}, u32[]{:S(2)}, u32[]{:S(2)}) collective-permute-start(f32[6,4,40,256]{3,2,1,0:T(8,128)} %bitcast.19), channel_id=1, source_target_pairs={{8,0},{16,8},{24,16},{32,24},{40,32},{48,40},{56,48},{64,56},{72,6... | collective-permute-start | bytes 2949128 | tf_op jit(solution)/shard_map/ppermute | solution.py:296
  80.3 9.9 %all-to-all-done.2 = f32[64,16,128]{2,1,0:T(8,128)S(1)} async-done(((f32[64,16,128]{2,1,0:T(8,128)}), f32[64,16,128]{2,1,0:T(8,128)S(1)}, u32[]{:S(2)}, u32[]{:S(2)}) %all-to-all-start.2) | async-done | bytes 524320 | tf_op jit(solution)/shard_map/all_to_all | solution.py:313
  91.0 3.4 %all-to-all-start.3 = ((f32[8,80,128]{2,1,0:T(8,128)}), f32[8,80,128]{2,1,0:T(8,128)S(1)}, u32[]{:S(2)}, u32[]{:S(2)}) async-start(f32[8,80,128]{2,1,0:T(8,128)} %bitcast.10), calls=%async_computation.3 | async-start | bytes 655360 | tf_op jit(solution)/shard_map/all_to_all | solution.py:313
  95.2 13.0 %all-to-all-done.3 = f32[8,80,128]{2,1,0:T(8,128)S(1)} async-done(((f32[8,80,128]{2,1,0:T(8,128)}), f32[8,80,128]{2,1,0:T(8,128)S(1)}, u32[]{:S(2)}, u32[]{:S(2)}) %all-to-all-start.3) | async-done | bytes 327712 | tf_op jit(solution)/shard_map/all_to_all | solution.py:313
  108.2 0.9 shard_map.189
  109.2 0.9 slice.26
  110.7 1.0 copy-done.2
  111.7 1.0 copy-done.3
  112.7 1.0 copy-done.4
  113.8 13.3 %shard_map.190 = f32[4,32,256]{2,1,0:T(8,128)} custom-call(s32[2]{0:T(128)S(1)} %pad_add_fusion.refs_0_, s32[1]{0:T(128)S(6)} %copy.35.refs_1_, s32[312]{0:T(512)S(1)} %reshape.58.refs_2_, f32[640,128]{1,0:T(8,128)S(1)} %bitcast.27, f32[6,4,40,256]{3,2,1,0:T(8,128)S(1)} %collective-permute-done.refs_4_, f32[8,4,40,256]{3,2,1,0:T(8,128)S(1)} %bitcast.25, ...), custom_call_target="tpu_custom_call" | custom-call | tf_op jit(solution)/shard_map/pallas_call | solution.py:379
  (43 shorter events, 3.1 us)
Async XLA Ops:
  7.2 27.0 %copy-start.7 = (bf16[384,384]{1,0:T(8,128)(2,1)S(1)}, bf16[384,384]{1,0:T(8,128)(2,1)}, u32[]{:S(2)}) copy-start(bf16[384,384]{1,0:T(8,128)(2,1)} %constant.86.clone.refs_1_) | copy-start | bytes 884740
  7.2 27.0 %copy-start.8 = (bf16[384,384]{1,0:T(8,128)(2,1)S(1)}, bf16[384,384]{1,0:T(8,128)(2,1)}, u32[]{:S(2)}) copy-start(bf16[384,384]{1,0:T(8,128)(2,1)} %constant.87.clone.refs_2_) | copy-start | bytes 884740
  7.2 64.6 %all-gather.3.cloned.1.call-start = ((), (), s32[]{:S(2)}) async-start(), calls=%async_computation.4 | async-start | bytes 1474560 | tf_op jit(solution)/shard_map/all_gather | solution.py:330
  9.6 0.9 copy-start.9
  10.5 0.9 copy-start.10
  11.4 0.9 copy-start.11
  12.3 0.9 copy-start.12
  13.2 0.9 copy-start.13
  14.1 33.9 %copy-start.15 = (s32[2048,6,3]{0,2,1:T(4,128)S(1)}, s32[2048,6,3]{0,2,1:T(4,128)}, u32[]{:S(2)}) copy-start(s32[2048,6,3]{0,2,1:T(4,128)} %param.22) | copy-start | bytes 442372
  14.5 46.6 %copy-start.5 = (bf16[512,512]{1,0:T(8,128)(2,1)S(1)}, bf16[512,512]{1,0:T(8,128)(2,1)}, u32[]{:S(2)}) copy-start(bf16[512,512]{1,0:T(8,128)(2,1)} %constant.88.clone.refs_3_) | copy-start | bytes 1572868
  14.6 46.6 %copy-start.6 = (bf16[512,512]{1,0:T(8,128)(2,1)S(1)}, bf16[512,512]{1,0:T(8,128)(2,1)}, u32[]{:S(2)}) copy-start(bf16[512,512]{1,0:T(8,128)(2,1)} %constant.89.clone.refs_4_) | copy-start | bytes 1572868
  35.4 25.7 %all-to-all-start.1 = ((f32[64,8,128]{2,1,0:T(8,128)}), f32[64,8,128]{2,1,0:T(8,128)S(1)}, u32[]{:S(2)}, u32[]{:S(2)}) async-start(f32[64,8,128]{2,1,0:T(8,128)} %bitcast.6), calls=%async_computation.1 | async-start | bytes 524288 | tf_op jit(solution)/shard_map/all_to_all | solution.py:313
  67.1 23.1 %all-to-all-start.2 = ((f32[64,16,128]{2,1,0:T(8,128)}), f32[64,16,128]{2,1,0:T(8,128)S(1)}, u32[]{:S(2)}, u32[]{:S(2)}) async-start(f32[64,16,128]{2,1,0:T(8,128)} %bitcast.8), calls=%async_computation.2 | async-start | bytes 1048576 | tf_op jit(solution)/shard_map/all_to_all | solution.py:313
  74.7 20.4 %copy-start = (f32[32,40,256]{2,1,0:T(8,128)S(1)}, f32[32,40,256]{2,1,0:T(8,128)}, u32[]{:S(2)}) copy-start(f32[32,40,256]{2,1,0:T(8,128)} %all-gather.3.cloned.1.call-done) | copy-start | bytes 3932164
  74.7 35.9 %copy-start.1 = (bf16[512,512]{1,0:T(8,128)(2,1)S(1)}, bf16[512,512]{1,0:T(8,128)(2,1)}, u32[]{:S(2)}) copy-start(bf16[512,512]{1,0:T(8,128)(2,1)} %constant.91.clone.refs_8_) | copy-start | bytes 1572868
  74.7 35.9 %copy-start.14 = (bf16[32,192]{1,0:T(8,128)(2,1)S(1)}, bf16[32,192]{1,0:T(8,128)(2,1)}, u32[]{:S(2)}) copy-start(bf16[32,192]{1,0:T(8,128)(2,1)} %constant.90.clone.refs_7_) | copy-start | bytes 36868
  74.7 34.4 %collective-permute-start = (f32[6,4,40,256]{3,2,1,0:T(8,128)}, f32[6,4,40,256]{3,2,1,0:T(8,128)S(1)}, u32[]{:S(2)}, u32[]{:S(2)}) collective-permute-start(f32[6,4,40,256]{3,2,1,0:T(8,128)} %bitcast.15), channel_id=1, source_target_pairs={{504,0},{0,8},{8,16},{16,24},{24,32},{32,40},{40,48},{48,56},{56,6... | collective-permute-start | bytes 2949128 | tf_op jit(solution)/shard_map/ppermute | solution.py:296
  78.4 30.8 %collective-permute-start.1 = (f32[6,4,40,256]{3,2,1,0:T(8,128)}, f32[6,4,40,256]{3,2,1,0:T(8,128)}, u32[]{:S(2)}, u32[]{:S(2)}) collective-permute-start(f32[6,4,40,256]{3,2,1,0:T(8,128)} %bitcast.19), channel_id=1, source_target_pairs={{8,0},{16,8},{24,16},{32,24},{40,32},{48,40},{56,48},{64,56},{72,6... | collective-permute-start | bytes 2949128 | tf_op jit(solution)/shard_map/ppermute | solution.py:296
  91.0 17.2 %all-to-all-start.3 = ((f32[8,80,128]{2,1,0:T(8,128)}), f32[8,80,128]{2,1,0:T(8,128)S(1)}, u32[]{:S(2)}, u32[]{:S(2)}) async-start(f32[8,80,128]{2,1,0:T(8,128)} %bitcast.10), calls=%async_computation.3 | async-start | bytes 655360 | tf_op jit(solution)/shard_map/all_to_all | solution.py:313
  110.6 1.0 copy-start.2
  111.7 1.0 copy-start.3
  112.7 1.0 copy-start.4
Sparse Core Ops, SparseCore 0:
  10.1 44.3 all-gather.2

commit v2 on v1

v2 whole, which is shorter than its diff:
```python
import jax
import jax.numpy as jnp
import ml_dtypes
import numpy as np
from jax import lax
from jax.experimental import pallas as pl
from jax.experimental.pallas import tpu as pltpu
from jax.sharding import PartitionSpec as P

SUBCYCLES = 2
PHASE_RATE = 8.0
TAYLOR_STEP = 0.6
EDGE = 16
CELLS = EDGE * EDGE
LANES = 128
REACH = 6
VMEM = pl.BlockSpec(memory_space=pltpu.VMEM)
SMEM = pl.BlockSpec(memory_space=pltpu.SMEM)
PARAMS = pltpu.CompilerParams(vmem_limit_bytes=48 * 2**20)
F32 = jnp.float32
BF16 = jnp.bfloat16


def two_parts(matrix):
    high = matrix.astype(ml_dtypes.bfloat16)
    low = (matrix - high.astype(np.float64)).astype(ml_dtypes.bfloat16)
    return high, low


def circulant(length):
    signed = np.fft.fftfreq(length, 1.0 / length)
    phase = np.exp(-1j * PHASE_RATE * (2.0 * np.pi * signed / length) ** 2)
    kernel = np.fft.ifft(phase)
    index = np.arange(length)
    matrix = kernel[(index[:, None] - index[None, :]) % length]
    return matrix.real, matrix.imag


def stacked(*matrices):
    return np.concatenate([part for m in matrices for part in two_parts(m)], 0)


def sweep_tables():
    laplace = -2.0 * np.eye(24) + np.eye(24, k=1) + np.eye(24, k=-1)
    squared = laplace @ laplace
    c = TAYLOR_STEP
    real = np.eye(24) - c**2 / 2.0 * squared + c**4 / 24.0 * squared @ squared
    imag = c * laplace - c**3 / 6.0 * squared @ laplace
    own, ghost, half = [], [], []
    for rows in (real[4:20], imag[4:20]):
        assert np.allclose(rows[:8, :16], rows[8:, 8:])
        edge = np.zeros((EDGE, EDGE))
        edge[:, 12:] = rows[:, :4]
        edge[:, :4] = rows[:, 20:]
        own.append(rows[:, 4:20])
        ghost.append(edge)
        half.append(np.concatenate([rows[:8, 4:16], rows[:8, :4]], 1))
    left = [np.block([[t[0], -t[1]], [t[1], t[0]]]) for t in (own, ghost)]
    high, low = two_parts(np.concatenate(left, 1))
    pad = np.zeros((2 * EDGE, CELLS - 12 * EDGE), high.dtype)
    left = np.concatenate([high, high, low, pad], 1)
    middle = np.concatenate([np.kron(t.T, np.eye(EDGE)) for t in half], 1)
    last = np.block([[np.kron(np.eye(8), t[i].T) for i in range(2)] for t in (own, ghost)])
    return np.concatenate([stacked(middle, last), left], 0)


def split(values):
    high = values.astype(BF16)
    return high, (values - high.astype(F32)).astype(BF16)


def halves(table_ref, index):
    size = table_ref.shape[1]
    start = 2 * size * index
    return table_ref[start : start + size, :], table_ref[start + size : start + 2 * size, :]


def mm(a, b):
    return jnp.dot(a, b, preferred_element_type=F32)


def mm3(a, b):
    return mm(a[0], b[0]) + (mm(a[1], b[0]) + mm(a[0], b[1]))


def packed(tiles):
    used = tiles[0].shape[1]
    room = LANES - used
    pad = jnp.zeros((tiles[0].shape[0], 2 * room - used), tiles[0].dtype)
    extra = [t[:, :room] for t in tiles[4:]] + [jnp.concatenate([t[:, room:], pad], 1) for t in tiles[4:]]
    return [jnp.concatenate([t, e], 1) for t, e in zip(tiles[:4], extra, strict=True)]


def unpacked(rows, used):
    room = LANES - used
    extra = [jnp.concatenate([rows[i][:, used:], rows[2 + i][:, used : 2 * used - room]], 1) for i in range(2)]
    return [t[:, :used] for t in rows] + extra


def along_last(rows_here, cols_here, parts, base_ref, near_ref, table_ref, out_ref):
    plane = rows_here * cols_here
    x = split(base_ref[...])
    pr = mm3(x, halves(table_ref, 0))
    pi = mm3(x, halves(table_ref, 1))
    done = (pr[:plane] - pi[plane:], pi[:plane] + pr[plane:])
    chunk = done[0].shape[1] // parts
    near = near_ref[...].astype(F32)
    near = jnp.concatenate([near, jnp.zeros((8 - near.shape[0], near.shape[1]), F32)], 0)
    free = LANES - cols_here // 8 * chunk
    near = jnp.concatenate([near, jnp.zeros((8, free - near.shape[1]), F32)], 1)
    pad = jnp.zeros((cols_here, LANES - (2 * rows_here - 1) * chunk), F32)
    for n in range(parts):
        pieces = [
            done[p][cols_here * x : cols_here * (x + 1), chunk * n : chunk * (n + 1)]
            for p in range(2)
            for x in range(rows_here)
        ]
        at = (cols_here + 8) * n
        out_ref[at : at + cols_here, :] = jnp.concatenate(pieces[:-1] + [pad], 1)
        last = [pieces[-1][8 * i : 8 * i + 8] for i in range(cols_here // 8)]
        out_ref[at + cols_here : at + cols_here + 8, :] = jnp.concatenate(last + [near], 1)


def along_second(rows_here, chunk, wide, narrow, x_ref, table_ref, out_ref):
    cols_here = x_ref.shape[0] // narrow - 8
    used = rows_here * chunk
    real = [x_ref[(cols_here + 8) * n : (cols_here + 8) * n + cols_here, :] for n in range(narrow)]
    real = jnp.concatenate(real, 0)
    last = []
    for n in range(narrow):
        tile = x_ref[(cols_here + 8) * n + cols_here : (cols_here + 8) * (n + 1), :]
        last += [tile[:, chunk * i : chunk * (i + 1)] for i in range(cols_here // 8)]
    last = jnp.concatenate(last, 0)
    pad = jnp.zeros((last.shape[0], LANES - used), F32)
    imag = jnp.concatenate([real[:, used : 2 * used - chunk], last, pad], 1)
    done = mm3(halves(table_ref, 0), split(jnp.concatenate([real, imag], 0)))
    tiles = []
    for p in range(2):
        for x in range(rows_here):
            pieces = [
                done[(p * rows_here + j) * wide : (p * rows_here + j + 1) * wide, chunk * x : chunk * (x + 1)]
                for j in range(rows_here)
            ]
            tiles.append(jnp.concatenate(pieces, 1))
    for q, row in enumerate(packed(tiles)):
        out_ref[pl.ds(q, wide, stride=4), :] = row


def plan(rows_here, chunk, wide, place_ref, cell_ref, line_ref, lane_ref, flag_ref):
    groups = cell_ref.shape[1]
    first = cell_ref[0:6, :]
    second = cell_ref[6:12, :] - place_ref[0] * rows_here
    last = cell_ref[12:18, :] - place_ref[1] * chunk
    mine = (second >= 0) & (second < rows_here) & (last >= 0) & (last < chunk)
    owner = first // rows_here
    lane = jnp.where(mine, second * chunk + last, -1)
    line_ref[0:6, :] = (first - owner * rows_here) * wide + owner
    lane_ref[0:6, :] = lane
    flag_ref[...] = jnp.full_like(flag_ref[...], -1)
    for c in range(groups // LANES):
        flag_ref[0:6, c : c + 1] = jnp.max(lane[:, LANES * c : LANES * (c + 1)], axis=1, keepdims=True)


def along_first(
    rows_here, chunk, wide, narrow, slots, flag_ref, line_ref, lane_ref, first_ref, x_ref, table_ref, out_ref, v_ref, left_ref
):
    used = rows_here * chunk
    lines = rows_here * wide
    groups = line_ref.shape[1]
    rows = [x_ref[pl.ds(q, wide, stride=4), :] for q in range(4)]
    blank = jnp.zeros((wide, LANES - used), F32)
    extra = [jnp.concatenate([t, blank], 1) for t in unpacked(rows, used)[4:]]
    done = mm3(halves(table_ref, 0), split(jnp.concatenate([x_ref[...]] + extra, 0)))
    turned = []
    for p in range(2):
        natural = [done[p * lines : (p + 1) * lines], jnp.zeros((256 - lines, LANES), F32)]
        turned.append(jnp.concatenate(natural, 0).T[:used])
    high, low = split(jnp.concatenate(turned, 0))
    left_ref[...] = jnp.concatenate([high, low], 0)
    v_ref[...] = jnp.zeros_like(v_ref[...])
    step = LANES

    def body(c, carry):
        at = pl.multiple_of(c * step, step)
        for f in range(6):

            @pl.when(flag_ref[f, c] >= 0)
            def _(f=f):
                line_of = lax.broadcasted_iota(jnp.int32, (256, step), 0)
                lane_of = lax.broadcasted_iota(jnp.int32, (used, step), 0)
                hot = jnp.where(line_of == line_ref[f : f + 1, pl.ds(at, step)], 1.0, 0.0).astype(BF16)
                taken = mm(left_ref[...], hot)
                keep = lane_of == lane_ref[f : f + 1, pl.ds(at, step)]
                for p in range(2):
                    both = taken[p * used : (p + 1) * used] + taken[(2 + p) * used : (3 + p) * used]
                    v_ref[4 + 6 * p + f : 5 + 6 * p + f, pl.ds(at + LANES, step)] = jnp.sum(
                        jnp.where(keep, both, 0.0), axis=0, keepdims=True
                    )

        return carry

    lax.fori_loop(0, groups // step, body, 0)
    v_ref[:, :LANES] = v_ref[:, groups : groups + LANES]
    v_ref[:, groups + LANES :] = v_ref[:, LANES : 2 * LANES]
    per_row = narrow * slots
    window = per_row + 10 * slots
    block = first_ref.shape[0] // narrow
    near = [
        first_ref[block * n + block - 8 : block * (n + 1), (block - 8) // 8 * chunk : (block - 8) // 8 * chunk + 6]
        for n in range(narrow)
    ]
    near = jnp.concatenate([t[:slots] for t in near], 1)
    near = jnp.concatenate([near, jnp.zeros((slots, LANES - window - near.shape[1]), F32)], 1)
    near = jnp.concatenate([jnp.zeros((4, LANES - window), F32), near, jnp.zeros((8, LANES - window), F32)], 0)
    for w in range(wide):
        start = LANES + w * per_row - 5 * slots
        out_ref[16 * w : 16 * w + 16, :] = jnp.concatenate([v_ref[:, start : start + window], near], 1)
    tiles = [done[wide * r : wide * (r + 1), :used] for r in range(2 * rows_here)]
    for q, row in enumerate(packed(tiles)):
        out_ref[pl.ds(q, wide, stride=16), :] = row


def forward_rows(slots, wide, narrow, place_ref, x_ref, out_ref, near_ref):
    per = wide // narrow
    block = 4 * per + 16
    low = jnp.zeros((8, LANES), F32)
    top = jnp.zeros((8, LANES), F32)
    for w in range(0, wide, 2):
        one = x_ref[16 * w : 16 * w + 8, :]
        two = x_ref[16 * w + 16 : 16 * w + 24, :]
        low += one + two
        top += x_ref[16 * w + 8 : 16 * w + 16, :] + x_ref[16 * w + 24 : 16 * w + 32, :]
        row = w // per * block + 4 * (w % per)
        out_ref[row : row + 8, :] = jnp.concatenate([one[:4], two[:4]], 0)
    for n in range(narrow):
        row = n * block + 4 * per
        out_ref[row : row + 8, :] = low
        out_ref[row + 8 : row + 16, :] = top
    devices = wide * narrow
    mine = place_ref[0] * narrow + place_ref[1]
    for o in range(3):
        at = lax.rem(place_ref[0] + (o - 1 + wide), wide) * 16
        numbers = x_ref[pl.ds(pl.multiple_of(at, 16), 8), :].astype(jnp.int32)
        owner = jnp.maximum(numbers, 0) // slots
        away = owner - mine + REACH
        away = jnp.where(away < 0, away + devices, away)
        away = jnp.where(away >= devices, away - devices, away)
        known = (numbers >= 0) & (away <= 2 * REACH)
        near_ref[8 * o : 8 * o + 8, :] = jnp.where(known, (away - owner) * slots + numbers, -1)


def unpack(rows_here, chunk, per, narrow, x_ref, out_ref, lo_ref, hi_ref):
    block = 4 * per + 16
    cols = per * rows_here
    length = out_ref.shape[1]
    tiles = [
        unpacked([x_ref[pl.ds(n * block + q, per, stride=4), :] for q in range(4)], rows_here * chunk)
        for n in range(narrow)
    ]
    for r in range(2 * rows_here):
        for y in range(rows_here):
            pieces = [t[r][:, chunk * y : chunk * (y + 1)] for t in tiles]
            line = jnp.concatenate(pieces + [jnp.zeros((per, 2 * LANES - length), F32)], 1)
            lo_ref[pl.ds(r * cols + y, per, stride=rows_here), :] = line[:, :LANES]
            hi_ref[pl.ds(r * cols + y, per, stride=rows_here), :] = line[:, LANES:]
    out_ref[:, :LANES] = lo_ref[...]
    out_ref[:, LANES:] = hi_ref[:, : length - LANES]


def sweeps(
    slots, narrow, per, used, place_ref, count_ref, near_ref, recv_ref, before_ref, row_ref, after_ref,
    table_ref, out_ref, one_ref, two_ref, edge_ref, edge_smem, sem,
):
    block = 4 * per + 16
    low = jnp.zeros((8, LANES), F32)
    top = jnp.zeros((8, LANES), F32)
    for n in range(narrow):
        row = n * block + 4 * per
        low += recv_ref[row : row + 8, :]
        top += recv_ref[row + 8 : row + 16, :]
    edge_ref[0:8, :] = low
    edge_ref[8:16, :] = top
    copy = pltpu.make_async_copy(edge_ref, edge_smem, sem)
    copy.start()
    mine = place_ref[1]
    total = 2 * REACH + 1
    for r in range(total):
        at = mine + r + narrow - REACH

        @pl.when(at < narrow)
        def _(r=r, at=at):
            one_ref[slots * r : slots * (r + 1)] = before_ref[at - (narrow - REACH)]

        @pl.when((at >= narrow) & (at < 2 * narrow))
        def _(r=r, at=at):
            one_ref[slots * r : slots * (r + 1)] = row_ref[at - narrow]

        @pl.when(at >= 2 * narrow)
        def _(r=r, at=at):
            one_ref[slots * r : slots * (r + 1)] = after_ref[at - 2 * narrow]

    copy.wait()
    row = lax.broadcasted_iota(jnp.int32, (2 * EDGE, CELLS), 0)
    real = row < EDGE
    late_row = row % EDGE >= 8
    column = lax.broadcasted_iota(jnp.int32, (2 * EDGE, LANES), 1)
    real_half = real[:, :LANES]
    early_half = column < LANES // 2
    late_last = column % EDGE >= 8
    left = table_ref[4 * CELLS :, : 12 * EDGE]
    held = [one_ref, two_ref]
    for s in range(3 * SUBCYCLES):
        k = s % 3
        source, target = held[s % 2], held[1 - s % 2]
        first, end = slots * (s + 1), slots * (total - s - 1)

        def ghost(q, face, part, is_real, source=source):
            at = q // slots + mine + narrow - REACH
            near = near_ref[at // narrow * 8 + 4 + q % slots, used + 6 * (at % narrow) + face]
            lane = q + slots * (mine - 1)
            flat = jnp.where(is_real, edge_smem[4 + face, lane], edge_smem[10 + face, lane])
            return jnp.where(near >= 0, source[jnp.maximum(near, 0), :, part], flat)

        if k == 0:

            def step(q, carry, source=source, target=target, ghost=ghost):
                every = slice(0, CELLS)
                around = jnp.where(late_row, ghost(q, 0, every, real), ghost(q, 1, every, real))
                high, rest = split(jnp.concatenate([source[q], around], 0))
                target[q] = mm(left, jnp.concatenate([high, rest, high], 0))
                return carry

            lax.fori_loop(first, end, step, 0, unroll=4)
        else:
            table = halves(table_ref, k - 1)

            def step(d, carry, k=k, source=source, target=target, ghost=ghost, table=table):
                lower, upper = slice(0, LANES), slice(LANES, CELLS)
                lines = []
                for i in range(slots):
                    q = slots * d + i
                    near, far = source[q, :, lower], source[q, :, upper]
                    if k == 1:
                        before = ghost(q, 2, upper, real_half)
                        after = ghost(q, 3, lower, real_half)
                        sides = jnp.where(early_half, far, before), jnp.where(early_half, after, near)
                    else:
                        sides = [
                            jnp.where(late_last, ghost(q, 4, part, real_half), ghost(q, 5, part, real_half))
                            for part in (lower, upper)
                        ]
                    lines += [jnp.concatenate([near, sides[0]], 1), jnp.concatenate([far, sides[1]], 1)]
                done = mm3(split(jnp.concatenate(lines, 0)), table)
                for i in range(slots):
                    for part, at in ((lower, 4 * EDGE * i), (upper, 4 * EDGE * i + 2 * EDGE)):
                        re, im = done[at : at + EDGE], done[at + EDGE : at + 2 * EDGE]
                        target[slots * d + i, 0:EDGE, part] = re[:, :LANES] - im[:, LANES:]
                        target[slots * d + i, EDGE:, part] = im[:, :LANES] + re[:, LANES:]
                return carry

            lax.fori_loop(first // slots, end // slots, step, 0)
    final = held[0]
    for i in range(slots):
        value = final[slots * REACH + i]
        out_ref[i] = jnp.where(i < count_ref[0], value, jnp.zeros_like(value))


def shifted(block, axis, distance):
    devices = range(lax.axis_size(axis))
    route = [((i - distance) % len(devices), i) for i in devices]
    return lax.ppermute(block, axis, route)


def call(kernel, outs, specs, scratch=()):
    return pl.pallas_call(
        kernel,
        out_shape=[jax.ShapeDtypeStruct(shape, dtype) for shape, dtype in outs],
        in_specs=specs,
        out_specs=[VMEM] * len(outs),
        scratch_shapes=list(scratch),
        compiler_params=PARAMS,
    )


def exchange(block, axis):
    parts = lax.axis_size(axis)
    shape = (parts, block.shape[0] // parts, block.shape[1])
    return lax.all_to_all(block.reshape(shape), axis, split_axis=0, concat_axis=0, tiled=True).reshape(block.shape)


def shards(base, fine_psi, counts, neighbors, base_cell):
    wide = lax.axis_size("wide")
    narrow = lax.axis_size("narrow")
    w_at = lax.axis_index("wide")
    n_at = lax.axis_index("narrow")
    _, rows_here, cols_here, length = base.shape
    slots = fine_psi.shape[0]
    chunk = length // narrow
    per = wide // narrow
    used = rows_here * chunk
    place = jnp.stack([w_at, n_at]).astype(jnp.int32)

    row = lax.all_gather(fine_psi.reshape(slots, 2 * EDGE, CELLS), "narrow", axis=0, tiled=False)
    before = shifted(row[narrow - REACH :], "wide", 1)
    after = shifted(row[:REACH], "wide", -1)

    kr, ki = circulant(length)
    (sent,) = call(
        lambda *refs: along_last(rows_here, cols_here, narrow, *refs),
        [((narrow * (cols_here + 8), LANES), F32)],
        [VMEM] * 3,
    )(base.reshape(2 * rows_here * cols_here, length), neighbors, jnp.asarray(stacked(kr, ki)))
    first = exchange(sent, "narrow")

    full = np.stack([np.stack([kr, -ki]), np.stack([ki, kr])])
    second = full.transpose(0, 2, 1, 3).reshape(2, wide, rows_here, 2 * length).transpose(0, 2, 1, 3)
    second = stacked(second.reshape(2 * length, 2 * length))
    (sent,) = call(
        lambda *refs: along_second(rows_here, chunk, wide, narrow, *refs), [((wide * 4, LANES), F32)], [VMEM] * 2
    )(first, jnp.asarray(second))
    groups = base_cell.shape[0]
    cells = jnp.transpose(base_cell, (2, 1, 0)).reshape(18, groups)
    line, lane, flags = call(
        lambda *refs: plan(rows_here, chunk, wide, *refs),
        [((8, groups), jnp.int32), ((8, groups), jnp.int32), ((8, LANES), jnp.int32)],
        [SMEM, VMEM],
    )(place, cells)

    got = exchange(sent, "wide")
    third = full.reshape(2, 2, wide, rows_here, wide, rows_here).transpose(0, 3, 2, 1, 5, 4)
    third = third.reshape(2 * length, 2 * rows_here, wide)
    main = third[:, :4].transpose(0, 2, 1).reshape(2 * length, 4 * wide)
    third = stacked(np.concatenate([main, third[:, 4:].reshape(2 * length, 2 * wide)], 1))
    (sent,) = call(
        lambda *refs: along_first(rows_here, chunk, wide, narrow, slots, *refs),
        [((wide * 16, LANES), F32)],
        [SMEM] + [VMEM] * 5,
        [pltpu.VMEM((16, groups + 2 * LANES), F32), pltpu.VMEM((4 * used, 256), BF16)],
    )(flags, line, lane, first, got, jnp.asarray(third))
    got = exchange(sent, "wide")
    sent, near = call(
        lambda *refs: forward_rows(slots, wide, narrow, *refs),
        [((narrow * (4 * per + 16), LANES), F32), ((24, LANES), jnp.int32)],
        [SMEM, VMEM],
    )(place, got)
    got = exchange(sent, "narrow")
    (drifted,) = call(
        lambda *refs: unpack(rows_here, chunk, per, narrow, *refs),
        [((2 * rows_here * cols_here, length), F32)],
        [VMEM],
        [pltpu.VMEM((2 * rows_here * cols_here, LANES), F32)] * 2,
    )(got)

    total = 2 * REACH + 1
    (fine,) = call(
        lambda *refs: sweeps(slots, narrow, per, used, *refs),
        [((slots, 2 * EDGE, CELLS), F32)],
        [SMEM] * 3 + [VMEM] * 5,
        [
            pltpu.VMEM((total * slots, 2 * EDGE, CELLS), F32),
            pltpu.VMEM((total * slots, 2 * EDGE, CELLS), F32),
            pltpu.VMEM((16, LANES), F32),
            pltpu.SMEM((16, LANES), F32),
            pltpu.SemaphoreType.DMA,
        ],
    )(place, counts, near, got, before, row, after, jnp.asarray(sweep_tables()))
    return (drifted.reshape(base.shape), fine.reshape(fine_psi.shape))


def solution(mesh):
    in_specs = (
        P(None, "wide", "narrow", None),
        P(("wide", "narrow"), None, None, None),
        P(("wide", "narrow")),
        P(("wide", "narrow"), None),
        P(),
    )
    out_specs = (P(None, "wide", "narrow", None), P(("wide", "narrow"), None, None, None))
    return jax.shard_map(shards, mesh=mesh, in_specs=in_specs, out_specs=out_specs, check_vma=False)
```

time: 135 us -> 125 us (0.926)
  local copies, waits for them, and re-layouts: 12.2 us -> 6.44 us
  waiting for transfers between devices: 35.8 us -> 31.2 us
  Pallas kernels: 22.6 us -> 25.2 us
  other arithmetic: 2.52 us -> 0.08 us
  starting transfers between devices: 26.3 us -> 27.9 us
    all_to_all x3, waiting for transfers between devices: 35.8 us -> 30.4 us  [exchange(): lax.all_to_all(block.reshape(shape), axis, split_axis=0, concat_axis=0, t...]
    unnamed x32 -> x16, local copies, waits for them, and re-layouts: 7.64 us -> 3.64 us
    pallas_call x1, Pallas kernels: 5.91 us -> 8.31 us  [shards(): call(lambda *refs: along_first(rows_here, chunk, wide, narrow, slots, *re...]
    concatenate x1 -> x0, other arithmetic: 1.58 us -> none  [shards(): jnp.concatenate([fine_psi.reshape(slots, 2 * EDGE, CELLS), numbers], 1)]
    all_to_all x3, starting transfers between devices: 20.7 us -> 22.2 us  [exchange(): lax.all_to_all(block.reshape(shape), axis, split_axis=0, concat_axis=0, t...]
    slice x4 -> x1, local copies, waits for them, and re-layouts: 3.83 us -> 2.68 us  [shards(): after = shifted(row[:REACH], 'wide', -1)]
    pallas_call x5 -> x6, Pallas kernels: 16.7 us -> 16.9 us  [the longest x1 12 us: shards(): call(lambda *refs: sweeps(slots, narrow, per, used, *refs), [((slots, 2 *...]
  transfers between devices with their start and end apart: 6 -> 6, of which waited for: 3 -> 3; matrix products, arithmetic and copies ran while one was open for 2% -> 2% of each run, Pallas kernels for 7% -> 11%
where the time goes in v2:
time: 125 us; the launch traced here: 124 us
  waiting for transfers between devices  31.2 us (25%)
  starting transfers between devices  27.9 us (22%)
  Pallas kernels  25.2 us (20%)
  blocking collectives  18.4 us (15%)
  between operations  14.8 us (12%)
  local copies, waits for them, and re-layouts  6.44 us (5%)
    all_to_all x3, waiting for transfers between devices, exchange(): lax.all_to_all(block.reshape(shape), axis, split_axis=0, concat_axis=0, t...  30.4 us
    all_to_all x3, starting transfers between devices, exchange(): lax.all_to_all(block.reshape(shape), axis, split_axis=0, concat_axis=0, t...  22.2 us
    all_to_all x1, blocking collectives, exchange(): lax.all_to_all(block.reshape(shape), axis, split_axis=0, concat_axis=0, t...  18.4 us
    pallas_call x1, Pallas kernels, shards(): call(lambda *refs: sweeps(slots, narrow, per, used, *refs), [((slots, 2 *...  12 us
    pallas_call x1, Pallas kernels, shards(): call(lambda *refs: along_first(rows_here, chunk, wide, narrow, slots, *re...  8.31 us
    ppermute x2, starting transfers between devices, shifted(): return lax.ppermute(block, axis, route)  5.58 us
    unnamed x16, local copies, waits for them, and re-layouts  3.64 us
    slice x1, local copies, waits for them, and re-layouts, shards(): after = shifted(row[:REACH], 'wide', -1)  2.68 us
  transfers between devices with their start and end apart: 6, of which 3 were waited for; matrix products, arithmetic and copies ran while one was open for 2% of the time, Pallas kernels for 11%

profile of v2, /device:TPU:1, one launch (start us, length us, event | category | flops | bytes accessed | tf_op | source)
XLA Modules:
  0.0 124.0 jit_solution(179338707078201110)
XLA Ops:
  7.2 0.7 all-gather.2.cloned.1.call-update
  7.9 1.0 copy-done.4
  8.9 0.9 copy-done.5
  9.8 0.7 copy-done.6
  10.5 0.5 shard_map.105
  11.0 18.4 %all_to_all.20 = f32[8,32,128]{2,1,0:T(8,128)S(1)} all-to-all(f32[8,32,128]{2,1,0:T(8,128)S(1)} %bitcast.21), channel_id=1, replica_groups=mesh['wide'=64,'narrow'=8] {'narrow'}, dimensions={0} | all-to-all | bytes 262144 | tf_op jit(solution)/shard_map/all_to_all | solution.py:388
  29.4 1.4 %shard_map.106 = f32[256,128]{1,0:T(8,128)} custom-call(f32[256,128]{1,0:T(8,128)S(1)} %bitcast.18, bf16[768,384]{1,0:T(8,128)(2,1)S(1)} %copy-done.1), custom_call_target="tpu_custom_call" | custom-call | tf_op jit(solution)/shard_map/pallas_call | solution.py:418
  30.8 12.5 %all-to-all-start.1 = ((f32[64,4,128]{2,1,0:T(4,128)}), f32[64,4,128]{2,1,0:T(4,128)S(1)}, u32[]{:S(2)}, u32[]{:S(2)}) async-start(f32[64,4,128]{2,1,0:T(4,128)} %bitcast.6), calls=%async_computation.1 | async-start | bytes 262144 | tf_op jit(solution)/shard_map/all_to_all | solution.py:388
  43.4 0.1 copy.12
  43.5 0.1 pad_add_fusion.refs_0_
  43.6 0.8 shard_map.104
  44.4 10.1 %all-to-all-done.1 = f32[64,4,128]{2,1,0:T(4,128)S(1)} async-done(((f32[64,4,128]{2,1,0:T(4,128)}), f32[64,4,128]{2,1,0:T(4,128)S(1)}, u32[]{:S(2)}, u32[]{:S(2)}) %all-to-all-start.1) | async-done | bytes 131104 | tf_op jit(solution)/shard_map/all_to_all | solution.py:388
  54.5 8.3 %shard_map.107 = f32[1024,128]{1,0:T(8,128)} custom-call(s32[8,128]{1,0:T(8,128)S(1)} %get-tuple-element.7.refs_0_, s32[8,2048]{1,0:T(8,128)S(1)} %get-tuple-element.8.refs_1_, s32[8,2048]{1,0:T(8,128)S(1)} %get-tuple-element.9.refs_2_, f32[256,128]{1,0:T(8,128)S(1)} %bitcast.19, f32[256,128]{1,0:T(8,128)S(1)} %bitcast.20, bf16[768,384]{1,0:T(8,128)(2,1)S(1)} %copy-done.2), custom_call_target="tpu_custom_call" | custom-call | tf_op jit(solution)/shard_map/pallas_call | solution.py:434
  62.8 6.3 %all-to-all-start.2 = ((f32[64,16,128]{2,1,0:T(8,128)}), f32[64,16,128]{2,1,0:T(8,128)S(1)}, u32[]{:S(2)}, u32[]{:S(2)}) async-start(f32[64,16,128]{2,1,0:T(8,128)} %bitcast.8), calls=%async_computation.2 | async-start | bytes 1048576 | tf_op jit(solution)/shard_map/all_to_all | solution.py:388
  69.1 2.7 %fusion = (f32[6,4,32,256]{3,2,1,0:T(8,128)}, f32[6,4,32,256]{3,2,1,0:T(8,128)}) fusion(f32[8,4,32,256]{3,2,1,0:T(8,128)} %all-gather.2.cloned.1.call-done.refs_5_), kind=kLoop, calls=%fused_computation.1 | loop fusion | bytes 3145728 | tf_op jit(solution)/shard_map/slice | solution.py:405
  71.8 3.7 %collective-permute-start = (f32[6,4,32,256]{3,2,1,0:T(8,128)}, f32[6,4,32,256]{3,2,1,0:T(8,128)S(1)}, u32[]{:S(2)}, u32[]{:S(2)}) collective-permute-start(f32[6,4,32,256]{3,2,1,0:T(8,128)} %get-tuple-element.13), channel_id=1, source_target_pairs={{504,0},{0,8},{8,16},{16,24},{24,32},{32,40},{40,48},{48,56},{56,6... | collective-permute-start | bytes 2359304 | tf_op jit(solution)/shard_map/ppermute | solution.py:371
  75.5 1.9 %collective-permute-start.1 = (f32[6,4,32,256]{3,2,1,0:T(8,128)}, f32[6,4,32,256]{3,2,1,0:T(8,128)S(1)}, u32[]{:S(2)}, u32[]{:S(2)}) collective-permute-start(f32[6,4,32,256]{3,2,1,0:T(8,128)} %get-tuple-element.12), channel_id=1, source_target_pairs={{8,0},{16,8},{24,16},{32,24},{40,32},{48,40},{56,48},{64,56},{72,6... | collective-permute-start | bytes 2359304 | tf_op jit(solution)/shard_map/ppermute | solution.py:371
  77.4 10.1 %all-to-all-done.2 = f32[64,16,128]{2,1,0:T(8,128)S(1)} async-done(((f32[64,16,128]{2,1,0:T(8,128)}), f32[64,16,128]{2,1,0:T(8,128)S(1)}, u32[]{:S(2)}, u32[]{:S(2)}) %all-to-all-start.2) | async-done | bytes 524320 | tf_op jit(solution)/shard_map/all_to_all | solution.py:388
  87.5 1.3 %shard_map.108 = (f32[384,128]{1,0:T(8,128)}, s32[24,128]{1,0:T(8,128)S(1)}) custom-call(s32[2]{0:T(128)S(1)} %pad_add_fusion.refs_0_, f32[1024,128]{1,0:T(8,128)S(1)} %bitcast.15), custom_call_target="tpu_custom_call" | custom-call | tf_op jit(solution)/shard_map/pallas_call | solution.py:441
  88.8 3.4 %all-to-all-start.3 = ((f32[8,48,128]{2,1,0:T(8,128)}), f32[8,48,128]{2,1,0:T(8,128)S(1)}, u32[]{:S(2)}, u32[]{:S(2)}) async-start(f32[8,48,128]{2,1,0:T(8,128)} %bitcast.10), calls=%async_computation.3 | async-start | bytes 393216 | tf_op jit(solution)/shard_map/all_to_all | solution.py:388
  92.8 10.3 %all-to-all-done.3 = f32[8,48,128]{2,1,0:T(8,128)S(1)} async-done(((f32[8,48,128]{2,1,0:T(8,128)}), f32[8,48,128]{2,1,0:T(8,128)S(1)}, u32[]{:S(2)}, u32[]{:S(2)}) %all-to-all-start.3) | async-done | bytes 196640 | tf_op jit(solution)/shard_map/all_to_all | solution.py:388
  103.1 0.9 shard_map.109
  104.1 1.0 copy-done.3
  105.1 12.0 %shard_map.110 = f32[4,32,256]{2,1,0:T(8,128)} custom-call(s32[2]{0:T(128)S(1)} %pad_add_fusion.refs_0_, s32[1]{0:T(128)S(6)} %copy.13.refs_1_, s32[24,128]{1,0:T(8,128)S(1)} %get-tuple-element.11.refs_2_, f32[384,128]{1,0:T(8,128)S(1)} %bitcast.17, f32[6,4,32,256]{3,2,1,0:T(8,128)S(1)} %collective-permute-done.refs_4_, f32[8,4,32,256]{3,2,1,0:T(8,128)S(1)} %copy-done, ...), custom_call_target="tpu_custom_call" | custom-call | tf_op jit(solution)/shard_map/pallas_call | solution.py:455
  (17 shorter events, 0.1 us)
Async XLA Ops:
  7.2 22.3 %copy-start.1 = (bf16[768,384]{1,0:T(8,128)(2,1)S(1)}, bf16[768,384]{1,0:T(8,128)(2,1)}, u32[]{:S(2)}) copy-start(bf16[768,384]{1,0:T(8,128)(2,1)} %constant.18.clone.refs_1_) | copy-start | bytes 1769476
  7.2 62.0 %all-gather.2.cloned.1.call-start = ((), (), s32[]{:S(2)}) async-start(), calls=%async_computation.4 | async-start | bytes 1179648 | tf_op jit(solution)/shard_map/all_gather | solution.py:403
  7.9 1.0 copy-start.4
  8.9 0.9 copy-start.5
  9.8 0.7 copy-start.6
  30.8 12.5 %copy-start.7 = (s32[2048,6,3]{0,2,1:T(4,128)S(1)}, s32[2048,6,3]{0,2,1:T(4,128)}, u32[]{:S(2)}) copy-start(s32[2048,6,3]{0,2,1:T(4,128)} %param.13) | copy-start | bytes 442372
  30.8 23.7 %copy-start.2 = (bf16[768,384]{1,0:T(8,128)(2,1)S(1)}, bf16[768,384]{1,0:T(8,128)(2,1)}, u32[]{:S(2)}) copy-start(bf16[768,384]{1,0:T(8,128)(2,1)} %constant.19.clone.refs_5_) | copy-start | bytes 1769476
  30.8 23.6 %all-to-all-start.1 = ((f32[64,4,128]{2,1,0:T(4,128)}), f32[64,4,128]{2,1,0:T(4,128)S(1)}, u32[]{:S(2)}, u32[]{:S(2)}) async-start(f32[64,4,128]{2,1,0:T(4,128)} %bitcast.6), calls=%async_computation.1 | async-start | bytes 262144 | tf_op jit(solution)/shard_map/all_to_all | solution.py:388
  62.8 24.7 %all-to-all-start.2 = ((f32[64,16,128]{2,1,0:T(8,128)}), f32[64,16,128]{2,1,0:T(8,128)S(1)}, u32[]{:S(2)}, u32[]{:S(2)}) async-start(f32[64,16,128]{2,1,0:T(8,128)} %bitcast.8), calls=%async_computation.2 | async-start | bytes 1048576 | tf_op jit(solution)/shard_map/all_to_all | solution.py:388
  71.8 32.2 %copy-start = (f32[8,4,32,256]{3,2,1,0:T(8,128)S(1)}, f32[8,4,32,256]{3,2,1,0:T(8,128)}, u32[]{:S(2)}) copy-start(f32[8,4,32,256]{3,2,1,0:T(8,128)} %all-gather.2.cloned.1.call-done.refs_5_) | copy-start | bytes 3145732
  71.8 32.2 %collective-permute-start = (f32[6,4,32,256]{3,2,1,0:T(8,128)}, f32[6,4,32,256]{3,2,1,0:T(8,128)S(1)}, u32[]{:S(2)}, u32[]{:S(2)}) collective-permute-start(f32[6,4,32,256]{3,2,1,0:T(8,128)} %get-tuple-element.13), channel_id=1, source_target_pairs={{504,0},{0,8},{8,16},{16,24},{24,32},{32,40},{40,48},{48,56},{56,6... | collective-permute-start | bytes 2359304 | tf_op jit(solution)/shard_map/ppermute | solution.py:371
  75.5 28.5 %collective-permute-start.1 = (f32[6,4,32,256]{3,2,1,0:T(8,128)}, f32[6,4,32,256]{3,2,1,0:T(8,128)S(1)}, u32[]{:S(2)}, u32[]{:S(2)}) collective-permute-start(f32[6,4,32,256]{3,2,1,0:T(8,128)} %get-tuple-element.12), channel_id=1, source_target_pairs={{8,0},{16,8},{24,16},{32,24},{40,32},{48,40},{56,48},{64,56},{72,6... | collective-permute-start | bytes 2359304 | tf_op jit(solution)/shard_map/ppermute | solution.py:371
  88.8 14.3 %all-to-all-start.3 = ((f32[8,48,128]{2,1,0:T(8,128)}), f32[8,48,128]{2,1,0:T(8,128)S(1)}, u32[]{:S(2)}, u32[]{:S(2)}) async-start(f32[8,48,128]{2,1,0:T(8,128)} %bitcast.10), calls=%async_computation.3 | async-start | bytes 393216 | tf_op jit(solution)/shard_map/all_to_all | solution.py:388
  104.0 1.1 copy-start.3
Sparse Core Ops, SparseCore 0:
  10.1 43.1 all-gather.1

commit v3 on v2

--- a/solution.py
+++ b/solution.py
@@ -146,60 +146,79 @@
         out_ref[pl.ds(q, wide, stride=4), :] = row
 
 
-def plan(rows_here, chunk, wide, place_ref, cell_ref, line_ref, lane_ref, flag_ref):
+def plan(rows_here, chunk, wide, place_ref, cell_ref, data_ref, upto_ref, count_ref):
     groups = cell_ref.shape[1]
     first = cell_ref[0:6, :]
     second = cell_ref[6:12, :] - place_ref[0] * rows_here
     last = cell_ref[12:18, :] - place_ref[1] * chunk
     mine = (second >= 0) & (second < rows_here) & (last >= 0) & (last < chunk)
     owner = first // rows_here
-    lane = jnp.where(mine, second * chunk + last, -1)
-    line_ref[0:6, :] = (first - owner * rows_here) * wide + owner
-    lane_ref[0:6, :] = lane
-    flag_ref[...] = jnp.full_like(flag_ref[...], -1)
-    for c in range(groups // LANES):
-        flag_ref[0:6, c : c + 1] = jnp.max(lane[:, LANES * c : LANES * (c + 1)], axis=1, keepdims=True)
+    lane = jnp.where(mine, second * chunk + last, -1).astype(F32)
+    line = ((first - owner * rows_here) * wide + owner).astype(F32)
+    pad = jnp.full((2, LANES), -1.0, F32)
+
+    def chunks(values):
+        parts = [values[:, LANES * c : LANES * (c + 1)] for c in range(groups // LANES)]
+        return jnp.concatenate([t for part in parts for t in (part, pad)], 0)
+
+    lane, line = chunks(lane), chunks(line)
+    mark = jnp.where(lane >= 0, 1.0, 0.0)
+    rows, size = mark.shape
+    earlier = lax.broadcasted_iota(jnp.int32, (size, size), 0) <= lax.broadcasted_iota(jnp.int32, (size, size), 1)
+    above = lax.broadcasted_iota(jnp.int32, (rows, rows), 1) <= lax.broadcasted_iota(jnp.int32, (rows, rows), 0)
+    in_row = mm(mark.astype(BF16), jnp.where(earlier, 1.0, 0.0).astype(BF16))
+    in_all = jnp.broadcast_to(jnp.sum(mark, axis=1, keepdims=True), mark.shape)
+    upto = mm(jnp.where(above, 1.0, 0.0).astype(BF16), in_all.astype(BF16))
+    high, low = split(upto - in_all + in_row)
+    upto_ref[...] = upto
+    count_ref[...] = upto[rows - 8 :].astype(jnp.int32)
+    data_ref[...] = jnp.concatenate([high, low] + [t.astype(BF16) for t in (mark, line, lane)], 1)
 
 
 def along_first(
-    rows_here, chunk, wide, narrow, slots, flag_ref, line_ref, lane_ref, first_ref, x_ref, table_ref, out_ref, v_ref, left_ref
+    rows_here, chunk, wide, narrow, slots, count_ref, data_ref, upto_ref, first_ref, x_ref, table_ref, out_ref, v_ref
 ):
     used = rows_here * chunk
     lines = rows_here * wide
-    groups = line_ref.shape[1]
+    faces = upto_ref.shape[0]
+    groups = faces // 8 * LANES
     rows = [x_ref[pl.ds(q, wide, stride=4), :] for q in range(4)]
     blank = jnp.zeros((wide, LANES - used), F32)
     extra = [jnp.concatenate([t, blank], 1) for t in unpacked(rows, used)[4:]]
     done = mm3(halves(table_ref, 0), split(jnp.concatenate([x_ref[...]] + extra, 0)))
-    turned = []
-    for p in range(2):
-        natural = [done[p * lines : (p + 1) * lines], jnp.zeros((256 - lines, LANES), F32)]
-        turned.append(jnp.concatenate(natural, 0).T[:used])
-    high, low = split(jnp.concatenate(turned, 0))
-    left_ref[...] = jnp.concatenate([high, low], 0)
+    parts = [split(done[p * lines : (p + 1) * lines]) for p in range(2)]
+    source = jnp.concatenate([parts[p][i] for i in range(2) for p in range(2)], 1)
     v_ref[...] = jnp.zeros_like(v_ref[...])
-    step = LANES
-
-    def body(c, carry):
-        at = pl.multiple_of(c * step, step)
-        for f in range(6):
-
-            @pl.when(flag_ref[f, c] >= 0)
-            def _(f=f):
-                line_of = lax.broadcasted_iota(jnp.int32, (256, step), 0)
-                lane_of = lax.broadcasted_iota(jnp.int32, (used, step), 0)
-                hot = jnp.where(line_of == line_ref[f : f + 1, pl.ds(at, step)], 1.0, 0.0).astype(BF16)
-                taken = mm(left_ref[...], hot)
-                keep = lane_of == lane_ref[f : f + 1, pl.ds(at, step)]
-                for p in range(2):
-                    both = taken[p * used : (p + 1) * used] + taken[(2 + p) * used : (3 + p) * used]
-                    v_ref[4 + 6 * p + f : 5 + 6 * p + f, pl.ds(at + LANES, step)] = jnp.sum(
-                        jnp.where(keep, both, 0.0), axis=0, keepdims=True
-                    )
-
+    shape = (LANES, LANES)
+    row_at = lax.broadcasted_iota(jnp.int32, (faces, LANES), 0)
+    deep = lax.broadcasted_iota(jnp.int32, (2 * faces, LANES), 0)
+    sub = lax.broadcasted_iota(jnp.int32, shape, 0)
+    lane_at = lax.broadcasted_iota(jnp.int32, shape, 1)
+    line_at = lax.broadcasted_iota(jnp.int32, (LANES, lines), 1)
+
+    def body(k, carry):
+        wanted = (lane_at[:1] + k * LANES).astype(F32)
+        row = jnp.sum(jnp.where(upto_ref[...] <= wanted, 1, 0), axis=0, keepdims=True)
+        hot = jnp.where(row_at == row, 1.0, 0.0).T.astype(BF16)
+        near = mm(hot, data_ref[...])
+        rank, mark, line, lane = near[:, :LANES] + near[:, LANES : 2 * LANES], *jnp.split(near[:, 2 * LANES :], 3, 1)
+        hit = jnp.where((rank == (sub + k * LANES + 1).astype(F32)) & (mark > 0.5), 1.0, 0.0)
+        line = jnp.sum(hit * line, axis=1, keepdims=True).astype(jnp.int32)
+        lane = jnp.sum(hit * lane, axis=1, keepdims=True).astype(jnp.int32)
+        taken = mm(jnp.where(line_at == line, 1.0, 0.0).astype(BF16), source)
+        back = []
+        for p in range(2):
+            both = taken[:, LANES * p : LANES * (p + 1)] + taken[:, LANES * (p + 2) : LANES * (p + 3)]
+            back.append(jnp.sum(jnp.where(lane_at == lane, both, 0.0), axis=1, keepdims=True) * hit)
+        high, low = split(jnp.concatenate(back, 0))
+        goal = row // 8 * 16 + row % 8 + 4
+        spread = jnp.concatenate([jnp.where(deep == goal + 6 * p, 1.0, 0.0).astype(BF16) for p in range(2)], 1)
+        values = mm(spread, high) + mm(spread, low)
+        for c in range(faces // 8):
+            v_ref[:, LANES * (c + 1) : LANES * (c + 2)] += values[16 * c : 16 * (c + 1)]
         return carry
 
-    lax.fori_loop(0, groups // step, body, 0)
+    lax.fori_loop(0, (count_ref[7, 0] + LANES - 1) // LANES, body, 0)
     v_ref[:, :LANES] = v_ref[:, groups : groups + LANES]
     v_ref[:, groups + LANES :] = v_ref[:, LANES : 2 * LANES]
     per_row = narrow * slots
@@ -420,9 +439,10 @@
     )(first, jnp.asarray(second))
     groups = base_cell.shape[0]
     cells = jnp.transpose(base_cell, (2, 1, 0)).reshape(18, groups)
-    line, lane, flags = call(
+    faces = groups // LANES * 8
+    data, upto, count = call(
         lambda *refs: plan(rows_here, chunk, wide, *refs),
-        [((8, groups), jnp.int32), ((8, groups), jnp.int32), ((8, LANES), jnp.int32)],
+        [((faces, 5 * LANES), BF16), ((faces, LANES), F32), ((8, LANES), jnp.int32)],
         [SMEM, VMEM],
     )(place, cells)
 
@@ -435,8 +455,8 @@
         lambda *refs: along_first(rows_here, chunk, wide, narrow, slots, *refs),
         [((wide * 16, LANES), F32)],
         [SMEM] + [VMEM] * 5,
-        [pltpu.VMEM((16, groups + 2 * LANES), F32), pltpu.VMEM((4 * used, 256), BF16)],
-    )(flags, line, lane, first, got, jnp.asarray(third))
+        [pltpu.VMEM((16, groups + 2 * LANES), F32)],
+    )(count, data, upto, first, got, jnp.asarray(third))
     got = exchange(sent, "wide")
     sent, near = call(
         lambda *refs: forward_rows(slots, wide, narrow, *refs),

time: 125 us -> 118 us (0.944)
  Pallas kernels: 25.2 us -> 20 us
  starting transfers between devices: 27.9 us -> 26 us
    pallas_call x1, Pallas kernels: 8.31 us -> 3 us  [shards(): call(lambda *refs: along_first(rows_here, chunk, wide, narrow, slots, *re...]
    all_to_all x3, starting transfers between devices: 22.2 us -> 20.4 us  [exchange(): lax.all_to_all(block.reshape(shape), axis, split_axis=0, concat_axis=0, t...]
  transfers between devices with their start and end apart: 6 -> 6, of which waited for: 3 -> 3; matrix products, arithmetic and copies ran while one was open for 2% -> 2% of each run, Pallas kernels for 11% -> 7%
where the time goes in v3:
time: 118 us; the launch traced here: 117 us
  waiting for transfers between devices  31.2 us (26%)
  starting transfers between devices  26 us (22%)
  Pallas kernels  20 us (17%)
  blocking collectives  18.4 us (16%)
  between operations  14.8 us (13%)
  local copies, waits for them, and re-layouts  6.44 us (5%)
    all_to_all x3, waiting for transfers between devices, exchange(): lax.all_to_all(block.reshape(shape), axis, split_axis=0, concat_axis=0, t...  30.5 us
    all_to_all x3, starting transfers between devices, exchange(): lax.all_to_all(block.reshape(shape), axis, split_axis=0, concat_axis=0, t...  20.4 us
    all_to_all x1, blocking collectives, exchange(): lax.all_to_all(block.reshape(shape), axis, split_axis=0, concat_axis=0, t...  18.4 us
    pallas_call x1, Pallas kernels, shards(): call(lambda *refs: sweeps(slots, narrow, per, used, *refs), [((slots, 2 *...  12 us
    ppermute x2, starting transfers between devices, shifted(): return lax.ppermute(block, axis, route)  5.59 us
    unnamed x16, local copies, waits for them, and re-layouts  3.64 us
    pallas_call x1, Pallas kernels, shards(): call(lambda *refs: along_first(rows_here, chunk, wide, narrow, slots, *re...  3 us
    slice x1, local copies, waits for them, and re-layouts, shards(): after = shifted(row[:REACH], 'wide', -1)  2.68 us
  transfers between devices with their start and end apart: 6, of which 3 were waited for; matrix products, arithmetic and copies ran while one was open for 2% of the time, Pallas kernels for 7%

profile of v3, /device:TPU:1, one launch (start us, length us, event | category | flops | bytes accessed | tf_op | source)
XLA Modules:
  0.0 117.0 jit_solution(608587870718992002)
XLA Ops:
  7.2 0.7 all-gather.2.cloned.1.call-update
  7.9 1.0 copy-done.4
  8.9 0.9 copy-done.5
  9.8 0.7 copy-done.6
  10.5 0.5 shard_map.105
  11.0 18.4 %all_to_all.20 = f32[8,32,128]{2,1,0:T(8,128)S(1)} all-to-all(f32[8,32,128]{2,1,0:T(8,128)S(1)} %bitcast.21), channel_id=1, replica_groups=mesh['wide'=64,'narrow'=8] {'narrow'}, dimensions={0} | all-to-all | bytes 262144 | tf_op jit(solution)/shard_map/all_to_all | solution.py:407
  29.4 1.4 %shard_map.106 = f32[256,128]{1,0:T(8,128)} custom-call(f32[256,128]{1,0:T(8,128)S(1)} %bitcast.18, bf16[768,384]{1,0:T(8,128)(2,1)S(1)} %copy-done.2), custom_call_target="tpu_custom_call" | custom-call | tf_op jit(solution)/shard_map/pallas_call | solution.py:437
  30.8 12.5 %all-to-all-start.1 = ((f32[64,4,128]{2,1,0:T(4,128)}), f32[64,4,128]{2,1,0:T(4,128)S(1)}, u32[]{:S(2)}, u32[]{:S(2)}) async-start(f32[64,4,128]{2,1,0:T(4,128)} %bitcast.6), calls=%async_computation.1 | async-start | bytes 262144 | tf_op jit(solution)/shard_map/all_to_all | solution.py:407
  43.4 0.1 copy.12
  43.5 0.1 pad_add_fusion.refs_0_
  43.6 0.9 shard_map.104
  44.5 10.0 %all-to-all-done.1 = f32[64,4,128]{2,1,0:T(4,128)S(1)} async-done(((f32[64,4,128]{2,1,0:T(4,128)}), f32[64,4,128]{2,1,0:T(4,128)S(1)}, u32[]{:S(2)}, u32[]{:S(2)}) %all-to-all-start.1) | async-done | bytes 131104 | tf_op jit(solution)/shard_map/all_to_all | solution.py:407
  54.5 3.0 %shard_map.107 = f32[1024,128]{1,0:T(8,128)} custom-call(s32[8,128]{1,0:T(8,128)S(1)} %get-tuple-element.7.refs_0_, bf16[128,640]{1,0:T(8,128)(2,1)S(1)} %get-tuple-element.8.refs_1_, f32[128,128]{1,0:T(8,128)S(1)} %get-tuple-element.9.refs_2_, f32[256,128]{1,0:T(8,128)S(1)} %bitcast.19, f32[256,128]{1,0:T(8,128)S(1)} %bitcast.20, bf16[768,384]{1,0:T(8,128)(2,1)S(1)} %copy-done.1), custom_call_target="tpu_custom_call" | custom-call | tf_op jit(solution)/shard_map/pallas_call | solution.py:454
  57.5 4.5 %all-to-all-start.2 = ((f32[64,16,128]{2,1,0:T(8,128)}), f32[64,16,128]{2,1,0:T(8,128)S(1)}, u32[]{:S(2)}, u32[]{:S(2)}) async-start(f32[64,16,128]{2,1,0:T(8,128)} %bitcast.8), calls=%async_computation.2 | async-start | bytes 1048576 | tf_op jit(solution)/shard_map/all_to_all | solution.py:407
  62.0 2.7 %fusion = (f32[6,4,32,256]{3,2,1,0:T(8,128)}, f32[6,4,32,256]{3,2,1,0:T(8,128)}) fusion(f32[8,4,32,256]{3,2,1,0:T(8,128)} %all-gather.2.cloned.1.call-done.refs_5_), kind=kLoop, calls=%fused_computation.1 | loop fusion | bytes 3145728 | tf_op jit(solution)/shard_map/slice | solution.py:424
  64.7 3.7 %collective-permute-start = (f32[6,4,32,256]{3,2,1,0:T(8,128)}, f32[6,4,32,256]{3,2,1,0:T(8,128)S(1)}, u32[]{:S(2)}, u32[]{:S(2)}) collective-permute-start(f32[6,4,32,256]{3,2,1,0:T(8,128)} %get-tuple-element.13), channel_id=1, source_target_pairs={{504,0},{0,8},{8,16},{16,24},{24,32},{32,40},{40,48},{48,56},{56,6... | collective-permute-start | bytes 2359304 | tf_op jit(solution)/shard_map/ppermute | solution.py:390
  68.3 1.9 %collective-permute-start.1 = (f32[6,4,32,256]{3,2,1,0:T(8,128)}, f32[6,4,32,256]{3,2,1,0:T(8,128)S(1)}, u32[]{:S(2)}, u32[]{:S(2)}) collective-permute-start(f32[6,4,32,256]{3,2,1,0:T(8,128)} %get-tuple-element.12), channel_id=1, source_target_pairs={{8,0},{16,8},{24,16},{32,24},{40,32},{48,40},{56,48},{64,56},{72,6... | collective-permute-start | bytes 2359304 | tf_op jit(solution)/shard_map/ppermute | solution.py:390
  70.3 10.2 %all-to-all-done.2 = f32[64,16,128]{2,1,0:T(8,128)S(1)} async-done(((f32[64,16,128]{2,1,0:T(8,128)}), f32[64,16,128]{2,1,0:T(8,128)S(1)}, u32[]{:S(2)}, u32[]{:S(2)}) %all-to-all-start.2) | async-done | bytes 524320 | tf_op jit(solution)/shard_map/all_to_all | solution.py:407
  80.5 1.3 %shard_map.108 = (f32[384,128]{1,0:T(8,128)}, s32[24,128]{1,0:T(8,128)S(1)}) custom-call(s32[2]{0:T(128)S(1)} %pad_add_fusion.refs_0_, f32[1024,128]{1,0:T(8,128)S(1)} %bitcast.15), custom_call_target="tpu_custom_call" | custom-call | tf_op jit(solution)/shard_map/pallas_call | solution.py:461
  81.8 3.4 %all-to-all-start.3 = ((f32[8,48,128]{2,1,0:T(8,128)}), f32[8,48,128]{2,1,0:T(8,128)S(1)}, u32[]{:S(2)}, u32[]{:S(2)}) async-start(f32[8,48,128]{2,1,0:T(8,128)} %bitcast.10), calls=%async_computation.3 | async-start | bytes 393216 | tf_op jit(solution)/shard_map/all_to_all | solution.py:407
  85.8 10.3 %all-to-all-done.3 = f32[8,48,128]{2,1,0:T(8,128)S(1)} async-done(((f32[8,48,128]{2,1,0:T(8,128)}), f32[8,48,128]{2,1,0:T(8,128)S(1)}, u32[]{:S(2)}, u32[]{:S(2)}) %all-to-all-start.3) | async-done | bytes 196640 | tf_op jit(solution)/shard_map/all_to_all | solution.py:407
  96.1 0.9 shard_map.109
  97.0 1.0 copy-done.3
  98.1 12.0 %shard_map.110 = f32[4,32,256]{2,1,0:T(8,128)} custom-call(s32[2]{0:T(128)S(1)} %pad_add_fusion.refs_0_, s32[1]{0:T(128)S(6)} %copy.13.refs_1_, s32[24,128]{1,0:T(8,128)S(1)} %get-tuple-element.11.refs_2_, f32[384,128]{1,0:T(8,128)S(1)} %bitcast.17, f32[6,4,32,256]{3,2,1,0:T(8,128)S(1)} %collective-permute-done.refs_4_, f32[8,4,32,256]{3,2,1,0:T(8,128)S(1)} %copy-done, ...), custom_call_target="tpu_custom_call" | custom-call | tf_op jit(solution)/shard_map/pallas_call | solution.py:475
  (17 shorter events, 0.1 us)
Async XLA Ops:
  7.2 22.3 %copy-start.2 = (bf16[768,384]{1,0:T(8,128)(2,1)S(1)}, bf16[768,384]{1,0:T(8,128)(2,1)}, u32[]{:S(2)}) copy-start(bf16[768,384]{1,0:T(8,128)(2,1)} %constant.18.clone.refs_1_) | copy-start | bytes 1769476
  7.2 54.8 %all-gather.2.cloned.1.call-start = ((), (), s32[]{:S(2)}) async-start(), calls=%async_computation.4 | async-start | bytes 1179648 | tf_op jit(solution)/shard_map/all_gather | solution.py:422
  7.9 1.0 copy-start.4
  8.9 0.9 copy-start.5
  9.8 0.7 copy-start.6
  30.8 12.5 %copy-start.7 = (s32[2048,6,3]{0,2,1:T(4,128)S(1)}, s32[2048,6,3]{0,2,1:T(4,128)}, u32[]{:S(2)}) copy-start(s32[2048,6,3]{0,2,1:T(4,128)} %param.13) | copy-start | bytes 442372
  30.8 23.7 %copy-start.1 = (bf16[768,384]{1,0:T(8,128)(2,1)S(1)}, bf16[768,384]{1,0:T(8,128)(2,1)}, u32[]{:S(2)}) copy-start(bf16[768,384]{1,0:T(8,128)(2,1)} %constant.19.clone.refs_5_) | copy-start | bytes 1769476
  30.8 23.6 %all-to-all-start.1 = ((f32[64,4,128]{2,1,0:T(4,128)}), f32[64,4,128]{2,1,0:T(4,128)S(1)}, u32[]{:S(2)}, u32[]{:S(2)}) async-start(f32[64,4,128]{2,1,0:T(4,128)} %bitcast.6), calls=%async_computation.1 | async-start | bytes 262144 | tf_op jit(solution)/shard_map/all_to_all | solution.py:407
  57.5 23.0 %all-to-all-start.2 = ((f32[64,16,128]{2,1,0:T(8,128)}), f32[64,16,128]{2,1,0:T(8,128)S(1)}, u32[]{:S(2)}, u32[]{:S(2)}) async-start(f32[64,16,128]{2,1,0:T(8,128)} %bitcast.8), calls=%async_computation.2 | async-start | bytes 1048576 | tf_op jit(solution)/shard_map/all_to_all | solution.py:407
  64.7 32.4 %copy-start = (f32[8,4,32,256]{3,2,1,0:T(8,128)S(1)}, f32[8,4,32,256]{3,2,1,0:T(8,128)}, u32[]{:S(2)}) copy-start(f32[8,4,32,256]{3,2,1,0:T(8,128)} %all-gather.2.cloned.1.call-done.refs_5_) | copy-start | bytes 3145732
  64.7 32.4 %collective-permute-start = (f32[6,4,32,256]{3,2,1,0:T(8,128)}, f32[6,4,32,256]{3,2,1,0:T(8,128)S(1)}, u32[]{:S(2)}, u32[]{:S(2)}) collective-permute-start(f32[6,4,32,256]{3,2,1,0:T(8,128)} %get-tuple-element.13), channel_id=1, source_target_pairs={{504,0},{0,8},{8,16},{16,24},{24,32},{32,40},{40,48},{48,56},{56,6... | collective-permute-start | bytes 2359304 | tf_op jit(solution)/shard_map/ppermute | solution.py:390
  68.3 28.7 %collective-permute-start.1 = (f32[6,4,32,256]{3,2,1,0:T(8,128)}, f32[6,4,32,256]{3,2,1,0:T(8,128)S(1)}, u32[]{:S(2)}, u32[]{:S(2)}) collective-permute-start(f32[6,4,32,256]{3,2,1,0:T(8,128)} %get-tuple-element.12), channel_id=1, source_target_pairs={{8,0},{16,8},{24,16},{32,24},{40,32},{48,40},{56,48},{64,56},{72,6... | collective-permute-start | bytes 2359304 | tf_op jit(solution)/shard_map/ppermute | solution.py:390
  81.8 14.3 %all-to-all-start.3 = ((f32[8,48,128]{2,1,0:T(8,128)}), f32[8,48,128]{2,1,0:T(8,128)S(1)}, u32[]{:S(2)}, u32[]{:S(2)}) async-start(f32[8,48,128]{2,1,0:T(8,128)} %bitcast.10), calls=%async_computation.3 | async-start | bytes 393216 | tf_op jit(solution)/shard_map/all_to_all | solution.py:407
  97.0 1.1 copy-start.3
Sparse Core Ops, SparseCore 0:
  10.1 43.1 all-gather.1

commit v4 on v3

--- a/solution.py
+++ b/solution.py
@@ -13,6 +13,7 @@
 EDGE = 16
 CELLS = EDGE * EDGE
 LANES = 128
+ROOM = 64
 REACH = 6
 VMEM = pl.BlockSpec(memory_space=pltpu.VMEM)
 SMEM = pl.BlockSpec(memory_space=pltpu.SMEM)
@@ -239,7 +240,7 @@
         out_ref[pl.ds(q, wide, stride=16), :] = row
 
 
-def forward_rows(slots, wide, narrow, place_ref, x_ref, out_ref, near_ref):
+def forward_rows(slots, wide, narrow, used, place_ref, x_ref, out_ref, near_ref):
     per = wide // narrow
     block = 4 * per + 16
     low = jnp.zeros((8, LANES), F32)
@@ -257,15 +258,56 @@
         out_ref[row + 8 : row + 16, :] = top
     devices = wide * narrow
     mine = place_ref[0] * narrow + place_ref[1]
+    tiles = []
     for o in range(3):
         at = lax.rem(place_ref[0] + (o - 1 + wide), wide) * 16
-        numbers = x_ref[pl.ds(pl.multiple_of(at, 16), 8), :].astype(jnp.int32)
-        owner = jnp.maximum(numbers, 0) // slots
-        away = owner - mine + REACH
-        away = jnp.where(away < 0, away + devices, away)
-        away = jnp.where(away >= devices, away - devices, away)
-        known = (numbers >= 0) & (away <= 2 * REACH)
-        near_ref[8 * o : 8 * o + 8, :] = jnp.where(known, (away - owner) * slots + numbers, -1)
+        tiles.append(x_ref[pl.ds(pl.multiple_of(at, 16), 8), used : used + 6 * narrow])
+    tiles.append(jnp.zeros((8, 2 * LANES - 18 * narrow), F32))
+    numbers = jnp.concatenate(tiles, 1).astype(jnp.int32)
+    owner = jnp.maximum(numbers, 0) // slots
+    away = owner - mine + REACH
+    away = jnp.where(away < 0, away + devices, away)
+    away = jnp.where(away >= devices, away - devices, away)
+    known = (numbers >= 0) & (away <= 2 * REACH)
+    near = jnp.where(known, (away - owner) * slots + numbers, -1)
+    shift = 2 * LANES - 6 * (place_ref[1] + narrow - REACH)
+    near_ref[...] = pltpu.roll(near, shift, 1)[:, :LANES]
+
+
+def needs(slots, count_ref, near_ref, list_ref, flag_ref):
+    total = (2 * REACH + 1) * slots
+    steps = 3 * SUBCYCLES
+
+    def clear(i, carry):
+        flag_ref[i] = 0
+        return carry
+
+    lax.fori_loop(0, (steps + 1) * ROOM, clear, 0, unroll=8)
+    for i in range(slots):
+        flag_ref[steps * ROOM + slots * REACH + i] = jnp.where(i < count_ref[0], 1, 0)
+    for s in reversed(range(steps)):
+        k = s % 3
+        base, before, after = 3 * ROOM * s, ROOM * s, ROOM * (s + 1)
+
+        def step(d, found, k=k, base=base, before=before, after=after):
+            for i in range(slots):
+                q = slots * d + i
+                need = flag_ref[after + q]
+                sides = [near_ref[4 + i, 6 * d + 2 * k + j] for j in range(2)]
+                list_ref[base + found] = q
+                list_ref[base + ROOM + found] = sides[0]
+                list_ref[base + 2 * ROOM + found] = sides[1]
+                flag_ref[before + jnp.where(need > 0, q, total)] = 1
+                for side in sides:
+                    flag_ref[before + jnp.where((need > 0) & (side >= 0), side, total)] = 1
+                found += need
+            return found
+
+        found = lax.fori_loop(s + 1, 2 * REACH - s, step, jnp.int32(0))
+        for i in range(slots):
+            for j in range(3):
+                list_ref[base + ROOM * j + found + i] = total
+        list_ref[3 * ROOM * steps + s] = found
 
 
 def unpack(rows_here, chunk, per, narrow, x_ref, out_ref, lo_ref, hi_ref):
@@ -287,7 +329,7 @@
 
 
 def sweeps(
-    slots, narrow, per, used, place_ref, count_ref, near_ref, recv_ref, before_ref, row_ref, after_ref,
+    slots, narrow, per, used, place_ref, count_ref, list_ref, recv_ref, before_ref, row_ref, after_ref,
     table_ref, out_ref, one_ref, two_ref, edge_ref, edge_smem, sem,
 ):
     block = 4 * per + 16
@@ -331,53 +373,58 @@
     for s in range(3 * SUBCYCLES):
         k = s % 3
         source, target = held[s % 2], held[1 - s % 2]
-        first, end = slots * (s + 1), slots * (total - s - 1)
-
-        def ghost(q, face, part, is_real, source=source):
-            at = q // slots + mine + narrow - REACH
-            near = near_ref[at // narrow * 8 + 4 + q % slots, used + 6 * (at % narrow) + face]
+        base = 3 * ROOM * s
+        rounds = (list_ref[3 * ROOM * 3 * SUBCYCLES + s] + slots - 1) // slots
+
+        def ghost(e, q, side, part, is_real, k=k, base=base, source=source):
+            near = list_ref[base + ROOM * (1 + side) + e]
             lane = q + slots * (mine - 1)
-            flat = jnp.where(is_real, edge_smem[4 + face, lane], edge_smem[10 + face, lane])
+            face = 4 + 2 * k + side
+            flat = jnp.where(is_real, edge_smem[face, lane], edge_smem[6 + face, lane])
             return jnp.where(near >= 0, source[jnp.maximum(near, 0), :, part], flat)
 
         if k == 0:
 
-            def step(q, carry, source=source, target=target, ghost=ghost):
+            def step(d, carry, base=base, source=source, target=target, ghost=ghost):
                 every = slice(0, CELLS)
-                around = jnp.where(late_row, ghost(q, 0, every, real), ghost(q, 1, every, real))
-                high, rest = split(jnp.concatenate([source[q], around], 0))
-                target[q] = mm(left, jnp.concatenate([high, rest, high], 0))
+                for i in range(slots):
+                    e = slots * d + i
+                    q = list_ref[base + e]
+                    around = jnp.where(late_row, ghost(e, q, 0, every, real), ghost(e, q, 1, every, real))
+                    high, rest = split(jnp.concatenate([source[q], around], 0))
+                    target[q] = mm(left, jnp.concatenate([high, rest, high], 0))
                 return carry
 
-            lax.fori_loop(first, end, step, 0, unroll=4)
         else:
             table = halves(table_ref, k - 1)
 
-            def step(d, carry, k=k, source=source, target=target, ghost=ghost, table=table):
+            def step(d, carry, k=k, base=base, source=source, target=target, ghost=ghost, table=table):
                 lower, upper = slice(0, LANES), slice(LANES, CELLS)
-                lines = []
+                lines, goals = [], []
                 for i in range(slots):
-                    q = slots * d + i
+                    e = slots * d + i
+                    q = list_ref[base + e]
+                    goals.append(q)
                     near, far = source[q, :, lower], source[q, :, upper]
                     if k == 1:
-                        before = ghost(q, 2, upper, real_half)
-                        after = ghost(q, 3, lower, real_half)
+                        before = ghost(e, q, 0, upper, real_half)
+                        after = ghost(e, q, 1, lower, real_half)
                         sides = jnp.where(early_half, far, before), jnp.where(early_half, after, near)
                     else:
                         sides = [
-                            jnp.where(late_last, ghost(q, 4, part, real_half), ghost(q, 5, part, real_half))
+                            jnp.where(late_last, ghost(e, q, 0, part, real_half), ghost(e, q, 1, part, real_half))
                             for part in (lower, upper)
                         ]
                     lines += [jnp.concatenate([near, sides[0]], 1), jnp.concatenate([far, sides[1]], 1)]
                 done = mm3(split(jnp.concatenate(lines, 0)), table)
-                for i in range(slots):
+                for i, q in enumerate(goals):
                     for part, at in ((lower, 4 * EDGE * i), (upper, 4 * EDGE * i + 2 * EDGE)):
                         re, im = done[at : at + EDGE], done[at + EDGE : at + 2 * EDGE]
-                        target[slots * d + i, 0:EDGE, part] = re[:, :LANES] - im[:, LANES:]
-                        target[slots * d + i, EDGE:, part] = im[:, :LANES] + re[:, LANES:]
+                        target[q, 0:EDGE, part] = re[:, :LANES] - im[:, LANES:]
+                        target[q, EDGE:, part] = im[:, :LANES] + re[:, LANES:]
                 return carry
 
-            lax.fori_loop(first // slots, end // slots, step, 0)
+        lax.fori_loop(0, rounds, step, 0)
     final = held[0]
     for i in range(slots):
         value = final[slots * REACH + i]
@@ -459,8 +506,8 @@
     )(count, data, upto, first, got, jnp.asarray(third))
     got = exchange(sent, "wide")
     sent, near = call(
-        lambda *refs: forward_rows(slots, wide, narrow, *refs),
-        [((narrow * (4 * per + 16), LANES), F32), ((24, LANES), jnp.int32)],
+        lambda *refs: forward_rows(slots, wide, narrow, used, *refs),
+        [((narrow * (4 * per + 16), LANES), F32), ((8, LANES), jnp.int32)],
         [SMEM, VMEM],
     )(place, got)
     got = exchange(sent, "narrow")
@@ -472,18 +519,27 @@
     )(got)
 
     total = 2 * REACH + 1
+    entries = 3 * SUBCYCLES * 3 * ROOM + LANES
+    lists = pl.pallas_call(
+        lambda *refs: needs(slots, *refs),
+        out_shape=jax.ShapeDtypeStruct((entries,), jnp.int32),
+        in_specs=[SMEM] * 2,
+        out_specs=SMEM,
+        scratch_shapes=[pltpu.SMEM(((3 * SUBCYCLES + 1) * ROOM,), jnp.int32)],
+        compiler_params=PARAMS,
+    )(counts, near)
     (fine,) = call(
         lambda *refs: sweeps(slots, narrow, per, used, *refs),
         [((slots, 2 * EDGE, CELLS), F32)],
         [SMEM] * 3 + [VMEM] * 5,
         [
-            pltpu.VMEM((total * slots, 2 * EDGE, CELLS), F32),
-            pltpu.VMEM((total * slots, 2 * EDGE, CELLS), F32),
+            pltpu.VMEM((total * slots + 1, 2 * EDGE, CELLS), F32),
+            pltpu.VMEM((total * slots + 1, 2 * EDGE, CELLS), F32),
             pltpu.VMEM((16, LANES), F32),
             pltpu.SMEM((16, LANES), F32),
             pltpu.SemaphoreType.DMA,
         ],
-    )(place, counts, near, got, before, row, after, jnp.asarray(sweep_tables()))
+    )(place, counts, lists, got, before, row, after, jnp.asarray(sweep_tables()))
     return (drifted.reshape(base.shape), fine.reshape(fine_psi.shape))
 
 

time: 118 us -> 111 us (0.941)
  waiting for transfers between devices: 31.2 us -> 27.8 us
  Pallas kernels: 20 us -> 17 us
    pallas_call x1, Pallas kernels: 12 us -> 5.61 us  [shards(): call(lambda *refs: sweeps(slots, narrow, per, used, *refs), [((slots, 2 *...]
    pallas_call x1 -> x2, Pallas kernels: 1.28 us -> 4.72 us  [the longest x1 3.38 us: shards(): pl.pallas_call(lambda *refs: needs(slots, *refs), out_shape=jax.ShapeDtyp...]
    all_to_all x3, waiting for transfers between devices: 30.5 us -> 27.1 us  [exchange(): lax.all_to_all(block.reshape(shape), axis, split_axis=0, concat_axis=0, t...]
  transfers between devices with their start and end apart: 6 -> 6, of which waited for: 3 -> 3; matrix products, arithmetic and copies ran while one was open for 2% -> 3% of each run, Pallas kernels for 7% -> 10%
where the time goes in v4:
time: 111 us
  waiting for transfers between devices  27.8 us (25%)
  starting transfers between devices  26 us (23%)
  blocking collectives  18.4 us (17%)
  Pallas kernels  17 us (15%)
  between operations  14.8 us (13%)
  local copies, waits for them, and re-layouts  6.44 us (6%)
    all_to_all x3, waiting for transfers between devices, exchange(): lax.all_to_all(block.reshape(shape), axis, split_axis=0, concat_axis=0, t...  27.1 us
    all_to_all x3, starting transfers between devices, exchange(): lax.all_to_all(block.reshape(shape), axis, split_axis=0, concat_axis=0, t...  20.4 us
    all_to_all x1, blocking collectives, exchange(): lax.all_to_all(block.reshape(shape), axis, split_axis=0, concat_axis=0, t...  18.4 us
    pallas_call x1, Pallas kernels, shards(): call(lambda *refs: sweeps(slots, narrow, per, used, *refs), [((slots, 2 *...  5.61 us
    ppermute x2, starting transfers between devices, shifted(): return lax.ppermute(block, axis, route)  5.59 us
    unnamed x16, local copies, waits for them, and re-layouts  3.64 us
    pallas_call x1, Pallas kernels, shards(): pl.pallas_call(lambda *refs: needs(slots, *refs), out_shape=jax.ShapeDtyp...  3.38 us
    pallas_call x1, Pallas kernels, shards(): call(lambda *refs: along_first(rows_here, chunk, wide, narrow, slots, *re...  3 us
  transfers between devices with their start and end apart: 6, of which 3 were waited for; matrix products, arithmetic and copies ran while one was open for 3% of the time, Pallas kernels for 10%

profile of v4, /device:TPU:1, one launch (start us, length us, event | category | flops | bytes accessed | tf_op | source)
XLA Modules:
  0.0 110.6 jit_solution(5911450060245025651)
XLA Ops:
  7.2 0.7 all-gather.2.cloned.1.call-update
  7.9 1.0 copy-done.4
  8.9 0.9 copy-done.5
  9.8 0.7 copy-done.6
  10.5 0.5 shard_map.105
  11.0 18.4 %all_to_all.20 = f32[8,32,128]{2,1,0:T(8,128)S(1)} all-to-all(f32[8,32,128]{2,1,0:T(8,128)S(1)} %bitcast.21), channel_id=1, replica_groups=mesh['wide'=64,'narrow'=8] {'narrow'}, dimensions={0} | all-to-all | bytes 262144 | tf_op jit(solution)/shard_map/all_to_all | solution.py:454
  29.4 1.4 %shard_map.106 = f32[256,128]{1,0:T(8,128)} custom-call(f32[256,128]{1,0:T(8,128)S(1)} %bitcast.18, bf16[768,384]{1,0:T(8,128)(2,1)S(1)} %copy-done.2), custom_call_target="tpu_custom_call" | custom-call | tf_op jit(solution)/shard_map/pallas_call | solution.py:484
  30.8 12.5 %all-to-all-start.1 = ((f32[64,4,128]{2,1,0:T(4,128)}), f32[64,4,128]{2,1,0:T(4,128)S(1)}, u32[]{:S(2)}, u32[]{:S(2)}) async-start(f32[64,4,128]{2,1,0:T(4,128)} %bitcast.6), calls=%async_computation.1 | async-start | bytes 262144 | tf_op jit(solution)/shard_map/all_to_all | solution.py:454
  43.4 0.1 copy.12
  43.6 0.9 shard_map.104
  44.5 10.0 %all-to-all-done.1 = f32[64,4,128]{2,1,0:T(4,128)S(1)} async-done(((f32[64,4,128]{2,1,0:T(4,128)}), f32[64,4,128]{2,1,0:T(4,128)S(1)}, u32[]{:S(2)}, u32[]{:S(2)}) %all-to-all-start.1) | async-done | bytes 131104 | tf_op jit(solution)/shard_map/all_to_all | solution.py:454
  54.5 3.0 %shard_map.107 = f32[1024,128]{1,0:T(8,128)} custom-call(s32[8,128]{1,0:T(8,128)S(1)} %get-tuple-element.7.refs_0_, bf16[128,640]{1,0:T(8,128)(2,1)S(1)} %get-tuple-element.8.refs_1_, f32[128,128]{1,0:T(8,128)S(1)} %get-tuple-element.9.refs_2_, f32[256,128]{1,0:T(8,128)S(1)} %bitcast.19, f32[256,128]{1,0:T(8,128)S(1)} %bitcast.20, bf16[768,384]{1,0:T(8,128)(2,1)S(1)} %copy-done.1), custom_call_target="tpu_custom_call" | custom-call | tf_op jit(solution)/shard_map/pallas_call | solution.py:501
  57.5 4.5 %all-to-all-start.2 = ((f32[64,16,128]{2,1,0:T(8,128)}), f32[64,16,128]{2,1,0:T(8,128)S(1)}, u32[]{:S(2)}, u32[]{:S(2)}) async-start(f32[64,16,128]{2,1,0:T(8,128)} %bitcast.8), calls=%async_computation.2 | async-start | bytes 1048576 | tf_op jit(solution)/shard_map/all_to_all | solution.py:454
  62.0 2.7 %fusion = (f32[6,4,32,256]{3,2,1,0:T(8,128)}, f32[6,4,32,256]{3,2,1,0:T(8,128)}) fusion(f32[8,4,32,256]{3,2,1,0:T(8,128)} %all-gather.2.cloned.1.call-done.refs_5_), kind=kLoop, calls=%fused_computation.1 | loop fusion | bytes 3145728 | tf_op jit(solution)/shard_map/slice | solution.py:471
  64.7 3.7 %collective-permute-start = (f32[6,4,32,256]{3,2,1,0:T(8,128)}, f32[6,4,32,256]{3,2,1,0:T(8,128)S(1)}, u32[]{:S(2)}, u32[]{:S(2)}) collective-permute-start(f32[6,4,32,256]{3,2,1,0:T(8,128)} %get-tuple-element.13), channel_id=1, source_target_pairs={{504,0},{0,8},{8,16},{16,24},{24,32},{32,40},{40,48},{48,56},{56,6... | collective-permute-start | bytes 2359304 | tf_op jit(solution)/shard_map/ppermute | solution.py:437
  68.3 1.9 %collective-permute-start.1 = (f32[6,4,32,256]{3,2,1,0:T(8,128)}, f32[6,4,32,256]{3,2,1,0:T(8,128)S(1)}, u32[]{:S(2)}, u32[]{:S(2)}) collective-permute-start(f32[6,4,32,256]{3,2,1,0:T(8,128)} %get-tuple-element.12), channel_id=1, source_target_pairs={{8,0},{16,8},{24,16},{32,24},{40,32},{48,40},{56,48},{64,56},{72,6... | collective-permute-start | bytes 2359304 | tf_op jit(solution)/shard_map/ppermute | solution.py:437
  70.3 10.2 %all-to-all-done.2 = f32[64,16,128]{2,1,0:T(8,128)S(1)} async-done(((f32[64,16,128]{2,1,0:T(8,128)}), f32[64,16,128]{2,1,0:T(8,128)S(1)}, u32[]{:S(2)}, u32[]{:S(2)}) %all-to-all-start.2) | async-done | bytes 524320 | tf_op jit(solution)/shard_map/all_to_all | solution.py:454
  80.5 1.3 %shard_map.108 = (f32[384,128]{1,0:T(8,128)}, s32[8,128]{1,0:T(8,128)S(1)}) custom-call(s32[2]{0:T(128)S(1)} %pad_add_fusion.refs_0_, f32[1024,128]{1,0:T(8,128)S(1)} %bitcast.15), custom_call_target="tpu_custom_call" | custom-call | tf_op jit(solution)/shard_map/pallas_call | solution.py:508
  81.8 3.4 %all-to-all-start.3 = ((f32[8,48,128]{2,1,0:T(8,128)}), f32[8,48,128]{2,1,0:T(8,128)S(1)}, u32[]{:S(2)}, u32[]{:S(2)}) async-start(f32[8,48,128]{2,1,0:T(8,128)} %bitcast.10), calls=%async_computation.3 | async-start | bytes 393216 | tf_op jit(solution)/shard_map/all_to_all | solution.py:454
  85.9 3.4 %shard_map.110.refs_2_ = s32[1280]{0:T(1024)S(1)} custom-call(s32[1]{0:T(128)S(6)} %copy.13.refs_0_.refs_1_, s32[8,128]{1,0:T(8,128)S(1)} %get-tuple-element.11.refs_1_), custom_call_target="tpu_custom_call" | custom-call | tf_op jit(solution)/shard_map/pallas_call | solution.py:523
  89.3 6.9 %all-to-all-done.3 = f32[8,48,128]{2,1,0:T(8,128)S(1)} async-done(((f32[8,48,128]{2,1,0:T(8,128)}), f32[8,48,128]{2,1,0:T(8,128)S(1)}, u32[]{:S(2)}, u32[]{:S(2)}) %all-to-all-start.3) | async-done | bytes 196640 | tf_op jit(solution)/shard_map/all_to_all | solution.py:454
  96.2 0.9 shard_map.109
  97.1 1.0 copy-done.3
  98.1 5.6 %shard_map.111 = f32[4,32,256]{2,1,0:T(8,128)} custom-call(s32[2]{0:T(128)S(1)} %pad_add_fusion.refs_0_, s32[1]{0:T(128)S(6)} %copy.13.refs_0_.refs_1_, s32[1280]{0:T(1024)S(1)} %shard_map.110.refs_2_, f32[384,128]{1,0:T(8,128)S(1)} %bitcast.17, f32[6,4,32,256]{3,2,1,0:T(8,128)S(1)} %collective-permute-done.refs_4_, f32[8,4,32,256]{3,2,1,0:T(8,128)S(1)} %copy-done, ...), custom_call_target="tpu_custom_call" | custom-call | tf_op jit(solution)/shard_map/pallas_call | solution.py:531
  (18 shorter events, 0.2 us)
Async XLA Ops:
  7.2 22.3 %copy-start.2 = (bf16[768,384]{1,0:T(8,128)(2,1)S(1)}, bf16[768,384]{1,0:T(8,128)(2,1)}, u32[]{:S(2)}) copy-start(bf16[768,384]{1,0:T(8,128)(2,1)} %constant.18.clone.refs_1_) | copy-start | bytes 1769476
  7.2 54.8 %all-gather.2.cloned.1.call-start = ((), (), s32[]{:S(2)}) async-start(), calls=%async_computation.4 | async-start | bytes 1179648 | tf_op jit(solution)/shard_map/all_gather | solution.py:469
  7.9 1.0 copy-start.4
  8.9 0.9 copy-start.5
  9.8 0.7 copy-start.6
  30.8 12.5 %copy-start.7 = (s32[2048,6,3]{0,2,1:T(4,128)S(1)}, s32[2048,6,3]{0,2,1:T(4,128)}, u32[]{:S(2)}) copy-start(s32[2048,6,3]{0,2,1:T(4,128)} %param.13) | copy-start | bytes 442372
  30.8 23.7 %copy-start.1 = (bf16[768,384]{1,0:T(8,128)(2,1)S(1)}, bf16[768,384]{1,0:T(8,128)(2,1)}, u32[]{:S(2)}) copy-start(bf16[768,384]{1,0:T(8,128)(2,1)} %constant.19.clone.refs_5_) | copy-start | bytes 1769476
  30.8 23.6 %all-to-all-start.1 = ((f32[64,4,128]{2,1,0:T(4,128)}), f32[64,4,128]{2,1,0:T(4,128)S(1)}, u32[]{:S(2)}, u32[]{:S(2)}) async-start(f32[64,4,128]{2,1,0:T(4,128)} %bitcast.6), calls=%async_computation.1 | async-start | bytes 262144 | tf_op jit(solution)/shard_map/all_to_all | solution.py:454
  57.5 23.0 %all-to-all-start.2 = ((f32[64,16,128]{2,1,0:T(8,128)}), f32[64,16,128]{2,1,0:T(8,128)S(1)}, u32[]{:S(2)}, u32[]{:S(2)}) async-start(f32[64,16,128]{2,1,0:T(8,128)} %bitcast.8), calls=%async_computation.2 | async-start | bytes 1048576 | tf_op jit(solution)/shard_map/all_to_all | solution.py:454
  64.7 32.4 %copy-start = (f32[8,4,32,256]{3,2,1,0:T(8,128)S(1)}, f32[8,4,32,256]{3,2,1,0:T(8,128)}, u32[]{:S(2)}) copy-start(f32[8,4,32,256]{3,2,1,0:T(8,128)} %all-gather.2.cloned.1.call-done.refs_5_) | copy-start | bytes 3145732
  64.7 32.4 %collective-permute-start = (f32[6,4,32,256]{3,2,1,0:T(8,128)}, f32[6,4,32,256]{3,2,1,0:T(8,128)S(1)}, u32[]{:S(2)}, u32[]{:S(2)}) collective-permute-start(f32[6,4,32,256]{3,2,1,0:T(8,128)} %get-tuple-element.13), channel_id=1, source_target_pairs={{504,0},{0,8},{8,16},{16,24},{24,32},{32,40},{40,48},{48,56},{56,6... | collective-permute-start | bytes 2359304 | tf_op jit(solution)/shard_map/ppermute | solution.py:437
  68.3 28.7 %collective-permute-start.1 = (f32[6,4,32,256]{3,2,1,0:T(8,128)}, f32[6,4,32,256]{3,2,1,0:T(8,128)S(1)}, u32[]{:S(2)}, u32[]{:S(2)}) collective-permute-start(f32[6,4,32,256]{3,2,1,0:T(8,128)} %get-tuple-element.12), channel_id=1, source_target_pairs={{8,0},{16,8},{24,16},{32,24},{40,32},{48,40},{56,48},{64,56},{72,6... | collective-permute-start | bytes 2359304 | tf_op jit(solution)/shard_map/ppermute | solution.py:437
  81.8 14.3 %all-to-all-start.3 = ((f32[8,48,128]{2,1,0:T(8,128)}), f32[8,48,128]{2,1,0:T(8,128)S(1)}, u32[]{:S(2)}, u32[]{:S(2)}) async-start(f32[8,48,128]{2,1,0:T(8,128)} %bitcast.10), calls=%async_computation.3 | async-start | bytes 393216 | tf_op jit(solution)/shard_map/all_to_all | solution.py:454
  97.1 1.1 copy-start.3
Sparse Core Ops, SparseCore 0:
  10.1 43.1 all-gather.1

commit v5 on v4

--- a/solution.py
+++ b/solution.py
@@ -17,7 +17,7 @@
 REACH = 6
 VMEM = pl.BlockSpec(memory_space=pltpu.VMEM)
 SMEM = pl.BlockSpec(memory_space=pltpu.SMEM)
-PARAMS = pltpu.CompilerParams(vmem_limit_bytes=48 * 2**20)
+PARAMS = pltpu.CompilerParams(vmem_limit_bytes=20 * 2**20)
 F32 = jnp.float32
 BF16 = jnp.bfloat16
 
@@ -347,18 +347,19 @@
     total = 2 * REACH + 1
     for r in range(total):
         at = mine + r + narrow - REACH
+        place = (r - REACH + 4) % narrow
 
         @pl.when(at < narrow)
-        def _(r=r, at=at):
-            one_ref[slots * r : slots * (r + 1)] = before_ref[at - (narrow - REACH)]
+        def _(r=r, place=place):
+            one_ref[slots * r : slots * (r + 1)] = before_ref[place]
 
         @pl.when((at >= narrow) & (at < 2 * narrow))
-        def _(r=r, at=at):
-            one_ref[slots * r : slots * (r + 1)] = row_ref[at - narrow]
+        def _(r=r, place=place):
+            one_ref[slots * r : slots * (r + 1)] = row_ref[place]
 
         @pl.when(at >= 2 * narrow)
-        def _(r=r, at=at):
-            one_ref[slots * r : slots * (r + 1)] = after_ref[at - 2 * narrow]
+        def _(r=r, place=place):
+            one_ref[slots * r : slots * (r + 1)] = after_ref[place]
 
     copy.wait()
     row = lax.broadcasted_iota(jnp.int32, (2 * EDGE, CELLS), 0)
@@ -466,9 +467,11 @@
     used = rows_here * chunk
     place = jnp.stack([w_at, n_at]).astype(jnp.int32)
 
-    row = lax.all_gather(fine_psi.reshape(slots, 2 * EDGE, CELLS), "narrow", axis=0, tiled=False)
-    before = shifted(row[narrow - REACH :], "wide", 1)
-    after = shifted(row[:REACH], "wide", -1)
+    patches = fine_psi.reshape(1, slots, 2 * EDGE, CELLS)
+    trio = jnp.concatenate([shifted(patches, "narrow", 1), patches, shifted(patches, "narrow", -1)], 0)
+    row = jnp.concatenate([shifted(trio, "narrow", 3), trio, shifted(trio[:2], "narrow", -3)], 0)
+    before = shifted(row, "wide", 1)
+    after = shifted(row, "wide", -1)
 
     kr, ki = circulant(length)
     (sent,) = call(

time: 111 us -> 103 us (0.928); the launches traced: 111 us -> 101 us
  starting transfers between devices: 26 us -> 52 us
  blocking collectives: 18.4 us -> 0 us
  between operations: 14.8 us -> 1.52 us
  local copies, waits for them, and re-layouts: 6.44 us -> 2.13 us
    ppermute x2 -> x6, starting transfers between devices: 5.59 us -> 26.7 us  [shifted(): return lax.ppermute(block, axis, route)]
    all_to_all x1 -> x0, blocking collectives: 18.4 us -> none  [exchange(): lax.all_to_all(block.reshape(shape), axis, split_axis=0, concat_axis=0, t...]
    all_to_all x3 -> x4, starting transfers between devices: 20.4 us -> 25.3 us  [exchange(): lax.all_to_all(block.reshape(shape), axis, split_axis=0, concat_axis=0, t...]
    slice x1 -> x0, local copies, waits for them, and re-layouts: 2.68 us -> none  [shards(): after = shifted(row[:REACH], 'wide', -1)]
    ppermute x2 -> x6, waiting for transfers between devices: 0.01 us -> 2.4 us  [shifted(): return lax.ppermute(block, axis, route)]
    unnamed x16 -> x20, local copies, waits for them, and re-layouts: 3.64 us -> 1.99 us
    all_to_all x3 -> x4, waiting for transfers between devices: 27.1 us -> 25.6 us  [exchange(): lax.all_to_all(block.reshape(shape), axis, split_axis=0, concat_axis=0, t...]
  transfers between devices with their start and end apart: 6 -> 10, of which waited for: 3 -> 5; matrix products, arithmetic and copies ran while one was open for 3% -> 0% of each run, Pallas kernels for 10% -> 12%
where the time goes in v5:
time: 103 us; the launch traced here: 101 us
  starting transfers between devices  52 us (50%)
  waiting for transfers between devices  28 us (27%)
  Pallas kernels  17.3 us (17%)
  local copies, waits for them, and re-layouts  2.13 us (2%)
  between operations  1.52 us (1%)
    ppermute x6, starting transfers between devices, shifted(): return lax.ppermute(block, axis, route)  26.7 us
    all_to_all x4, waiting for transfers between devices, exchange(): lax.all_to_all(block.reshape(shape), axis, split_axis=0, concat_axis=0, t...  25.6 us
    all_to_all x4, starting transfers between devices, exchange(): lax.all_to_all(block.reshape(shape), axis, split_axis=0, concat_axis=0, t...  25.3 us
    pallas_call x1, Pallas kernels, shards(): call(lambda *refs: sweeps(slots, narrow, per, used, *refs), [((slots, 2 *...  5.17 us
    pallas_call x1, Pallas kernels, shards(): pl.pallas_call(lambda *refs: needs(slots, *refs), out_shape=jax.ShapeDtyp...  3.38 us
    pallas_call x1, Pallas kernels, shards(): call(lambda *refs: along_first(rows_here, chunk, wide, narrow, slots, *re...  3.01 us
    ppermute x6, waiting for transfers between devices, shifted(): return lax.ppermute(block, axis, route)  2.4 us
  transfers between devices with their start and end apart: 10, of which 5 were waited for; matrix products, arithmetic and copies ran while one was open for 0% of the time, Pallas kernels for 12%

profile of v5, /device:TPU:1, one launch (start us, length us, event | category | flops | bytes accessed | tf_op | source)
XLA Modules:
  0.0 101.0 jit_solution(15358152776696769413)
XLA Ops:
  0.6 11.5 %collective-permute-start.1 = (f32[1,4,32,256]{3,2,1,0:T(8,128)}, f32[1,4,32,256]{3,2,1,0:T(8,128)S(1)}, u32[]{:S(2)}, u32[]{:S(2)}) collective-permute-start(f32[1,4,32,256]{3,2,1,0:T(8,128)} %bitcast.22), channel_id=1, source_target_pairs={{1,0},{2,1},{3,2},{4,3},{5,4},{6,5},{7,6},{0,7},{9,8},{10,9},{11,1... | collective-permute-start | bytes 393224 | tf_op jit(solution)/shard_map/ppermute | solution.py:438
  12.1 1.9 %collective-permute-start = (f32[1,4,32,256]{3,2,1,0:T(8,128)}, f32[1,4,32,256]{3,2,1,0:T(8,128)S(1)}, u32[]{:S(2)}, u32[]{:S(2)}) collective-permute-start(f32[1,4,32,256]{3,2,1,0:T(8,128)} %bitcast.23), channel_id=1, source_target_pairs={{7,0},{0,1},{1,2},{2,3},{3,4},{4,5},{5,6},{6,7},{15,8},{8,9},{9,10... | collective-permute-start | bytes 393224 | tf_op jit(solution)/shard_map/ppermute | solution.py:438
  14.1 1.0 copy-done.3
  16.0 1.1 %shard_map.105 = f32[256,128]{1,0:T(8,128)} custom-call(f32[144,192]{1,0:T(8,128)S(1)} %bitcast.21, s32[4,6]{1,0:T(4,128)S(1)} %copy-done.5, bf16[768,192]{1,0:T(8,128)(2,1)S(1)} %copy-done.3), custom_call_target="tpu_custom_call" | custom-call | tf_op jit(solution)/shard_map/pallas_call | solution.py:477
  17.1 4.1 %all-to-all-start = ((f32[8,32,128]{2,1,0:T(8,128)}), f32[8,32,128]{2,1,0:T(8,128)S(1)}, u32[]{:S(2)}, u32[]{:S(2)}) async-start(f32[8,32,128]{2,1,0:T(8,128)} %bitcast.4), calls=%async_computation | async-start | bytes 262144 | tf_op jit(solution)/shard_map/all_to_all | solution.py:455
  21.3 5.2 %collective-permute-start.2 = (f32[3,4,32,256]{3,2,1,0:T(8,128)S(1)}, f32[3,4,32,256]{3,2,1,0:T(8,128)S(1)}, u32[]{:S(2)}, u32[]{:S(2)}) collective-permute-start(f32[3,4,32,256]{3,2,1,0:T(8,128)S(1)} %pad_maximum_fusion), channel_id=1, source_target_pairs={{5,0},{6,1},{7,2},{0,3},{1,4},{2,5},{3,6},{4,7},{13,8},{14,9},{15,... | collective-permute-start | bytes 1179656 | tf_op jit(solution)/shard_map/ppermute | solution.py:438
  26.4 2.8 %all-to-all-done = f32[8,32,128]{2,1,0:T(8,128)S(1)} async-done(((f32[8,32,128]{2,1,0:T(8,128)}), f32[8,32,128]{2,1,0:T(8,128)S(1)}, u32[]{:S(2)}, u32[]{:S(2)}) %all-to-all-start) | async-done | bytes 131104 | tf_op jit(solution)/shard_map/all_to_all | solution.py:455
  29.3 1.4 %shard_map.106 = f32[256,128]{1,0:T(8,128)} custom-call(f32[256,128]{1,0:T(8,128)S(1)} %bitcast.18, bf16[768,384]{1,0:T(8,128)(2,1)S(1)} %copy-done.1), custom_call_target="tpu_custom_call" | custom-call | tf_op jit(solution)/shard_map/pallas_call | solution.py:487
  30.7 13.4 %all-to-all-start.1 = ((f32[64,4,128]{2,1,0:T(4,128)}), f32[64,4,128]{2,1,0:T(4,128)S(1)}, u32[]{:S(2)}, u32[]{:S(2)}) async-start(f32[64,4,128]{2,1,0:T(4,128)} %bitcast.6), calls=%async_computation.1 | async-start | bytes 262144 | tf_op jit(solution)/shard_map/all_to_all | solution.py:455
  44.3 0.9 shard_map.104
  45.3 1.9 %collective-permute-start.3 = (f32[2,4,32,256]{3,2,1,0:T(8,128)S(1)}, f32[2,4,32,256]{3,2,1,0:T(8,128)S(1)}, u32[]{:S(2)}, u32[]{:S(2)}) collective-permute-start(f32[2,4,32,256]{3,2,1,0:T(8,128)S(1)} %pad_maximum_fusion.1), channel_id=1, source_target_pairs={{3,0},{4,1},{5,2},{6,3},{7,4},{0,5},{1,6},{2,7},{11,8},{12,9},{13,... | collective-permute-start | bytes 786440 | tf_op jit(solution)/shard_map/ppermute | solution.py:438
  47.2 8.0 %all-to-all-done.1 = f32[64,4,128]{2,1,0:T(4,128)S(1)} async-done(((f32[64,4,128]{2,1,0:T(4,128)}), f32[64,4,128]{2,1,0:T(4,128)S(1)}, u32[]{:S(2)}, u32[]{:S(2)}) %all-to-all-start.1) | async-done | bytes 131104 | tf_op jit(solution)/shard_map/all_to_all | solution.py:455
  55.2 3.0 %shard_map.107 = f32[1024,128]{1,0:T(8,128)} custom-call(s32[8,128]{1,0:T(8,128)S(1)} %get-tuple-element.7.refs_0_, bf16[128,640]{1,0:T(8,128)(2,1)S(1)} %get-tuple-element.8.refs_1_, f32[128,128]{1,0:T(8,128)S(1)} %get-tuple-element.9.refs_2_, f32[256,128]{1,0:T(8,128)S(1)} %bitcast.19, f32[256,128]{1,0:T(8,128)S(1)} %bitcast.20, bf16[768,384]{1,0:T(8,128)(2,1)S(1)} %copy-done), custom_call_target="tpu_custom_call" | custom-call | tf_op jit(solution)/shard_map/pallas_call | solution.py:504
  58.2 4.5 %all-to-all-start.2 = ((f32[64,16,128]{2,1,0:T(8,128)}), f32[64,16,128]{2,1,0:T(8,128)S(1)}, u32[]{:S(2)}, u32[]{:S(2)}) async-start(f32[64,16,128]{2,1,0:T(8,128)} %bitcast.8), calls=%async_computation.2 | async-start | bytes 1048576 | tf_op jit(solution)/shard_map/all_to_all | solution.py:455
  62.8 2.4 %collective-permute-done.3 = f32[2,4,32,256]{3,2,1,0:T(8,128)S(1)} collective-permute-done((f32[2,4,32,256]{3,2,1,0:T(8,128)S(1)}, f32[2,4,32,256]{3,2,1,0:T(8,128)S(1)}, u32[]{:S(2)}, u32[]{:S(2)}) %collective-permute-start.3) | collective-permute-done | bytes 262176 | tf_op jit(solution)/shard_map/ppermute | solution.py:438
  65.2 3.0 %collective-permute-start.5 = (f32[8,4,32,256]{3,2,1,0:T(8,128)S(1)}, f32[8,4,32,256]{3,2,1,0:T(8,128)S(1)}, u32[]{:S(2)}, u32[]{:S(2)}) collective-permute-start(f32[8,4,32,256]{3,2,1,0:T(8,128)S(1)} %constant_dynamic-update-slice_fusion.refs_5_), channel_id=1, source_target_pairs={{8,0},{16,8},{24,16},{32,24},{40,32},{48,40},{56,48},{64,56},{72,6... | collective-permute-start | bytes 3145736 | tf_op jit(solution)/shard_map/ppermute | solution.py:438
  68.2 3.2 %collective-permute-start.4 = (f32[8,4,32,256]{3,2,1,0:T(8,128)S(1)}, f32[8,4,32,256]{3,2,1,0:T(8,128)}, u32[]{:S(2)}, u32[]{:S(2)}) collective-permute-start(f32[8,4,32,256]{3,2,1,0:T(8,128)S(1)} %constant_dynamic-update-slice_fusion.refs_5_), channel_id=1, source_target_pairs={{504,0},{0,8},{8,16},{16,24},{24,32},{32,40},{40,48},{48,56},{56,6... | collective-permute-start | bytes 3145736 | tf_op jit(solution)/shard_map/ppermute | solution.py:438
  71.4 9.2 %all-to-all-done.2 = f32[64,16,128]{2,1,0:T(8,128)S(1)} async-done(((f32[64,16,128]{2,1,0:T(8,128)}), f32[64,16,128]{2,1,0:T(8,128)S(1)}, u32[]{:S(2)}, u32[]{:S(2)}) %all-to-all-start.2) | async-done | bytes 524320 | tf_op jit(solution)/shard_map/all_to_all | solution.py:455
  80.6 1.3 %shard_map.108 = (f32[384,128]{1,0:T(8,128)}, s32[8,128]{1,0:T(8,128)S(1)}) custom-call(s32[2]{0:T(128)S(1)} %pad_add_fusion.refs_0_, f32[1024,128]{1,0:T(8,128)S(1)} %bitcast.15), custom_call_target="tpu_custom_call" | custom-call | tf_op jit(solution)/shard_map/pallas_call | solution.py:511
  82.0 3.4 %all-to-all-start.3 = ((f32[8,48,128]{2,1,0:T(8,128)}), f32[8,48,128]{2,1,0:T(8,128)S(1)}, u32[]{:S(2)}, u32[]{:S(2)}) async-start(f32[8,48,128]{2,1,0:T(8,128)} %bitcast.10), calls=%async_computation.3 | async-start | bytes 393216 | tf_op jit(solution)/shard_map/all_to_all | solution.py:455
  86.0 3.4 %shard_map.110.refs_2_ = s32[1280]{0:T(1024)S(1)} custom-call(s32[1]{0:T(128)S(6)} %copy.16.refs_0_.refs_1_, s32[8,128]{1,0:T(8,128)S(1)} %get-tuple-element.11.refs_1_), custom_call_target="tpu_custom_call" | custom-call | tf_op jit(solution)/shard_map/pallas_call | solution.py:526
  89.4 5.5 %all-to-all-done.3 = f32[8,48,128]{2,1,0:T(8,128)S(1)} async-done(((f32[8,48,128]{2,1,0:T(8,128)}), f32[8,48,128]{2,1,0:T(8,128)S(1)}, u32[]{:S(2)}, u32[]{:S(2)}) %all-to-all-start.3) | async-done | bytes 196640 | tf_op jit(solution)/shard_map/all_to_all | solution.py:455
  94.9 0.9 shard_map.109
  95.9 5.2 %shard_map.111 = f32[4,32,256]{2,1,0:T(8,128)} custom-call(s32[2]{0:T(128)S(1)} %pad_add_fusion.refs_0_, s32[1]{0:T(128)S(6)} %copy.16.refs_0_.refs_1_, s32[1280]{0:T(1024)S(1)} %shard_map.110.refs_2_, f32[384,128]{1,0:T(8,128)S(1)} %bitcast.17, f32[8,4,32,256]{3,2,1,0:T(8,128)} %collective-permute-done.4.refs_4_, ...), custom_call_target="tpu_custom_call" | custom-call | tf_op jit(solution)/shard_map/pallas_call | solution.py:534
  (30 shorter events, 1.3 us)
Async XLA Ops:
  0.6 13.4 %copy-start.5 = (s32[4,6]{1,0:T(4,128)S(1)}, s32[4,6]{1,0:T(4,128)}, u32[]{:S(2)}) copy-start(s32[4,6]{1,0:T(4,128)} %refs_1_.3) | copy-start | bytes 292
  0.6 20.6 %collective-permute-start.1 = (f32[1,4,32,256]{3,2,1,0:T(8,128)}, f32[1,4,32,256]{3,2,1,0:T(8,128)S(1)}, u32[]{:S(2)}, u32[]{:S(2)}) collective-permute-start(f32[1,4,32,256]{3,2,1,0:T(8,128)} %bitcast.22), channel_id=1, source_target_pairs={{1,0},{2,1},{3,2},{4,3},{5,4},{6,5},{7,6},{0,7},{9,8},{10,9},{11,1... | collective-permute-start | bytes 393224 | tf_op jit(solution)/shard_map/ppermute | solution.py:438
  12.1 9.1 %collective-permute-start = (f32[1,4,32,256]{3,2,1,0:T(8,128)}, f32[1,4,32,256]{3,2,1,0:T(8,128)S(1)}, u32[]{:S(2)}, u32[]{:S(2)}) collective-permute-start(f32[1,4,32,256]{3,2,1,0:T(8,128)} %bitcast.23), channel_id=1, source_target_pairs={{7,0},{0,1},{1,2},{2,3},{3,4},{4,5},{5,6},{6,7},{15,8},{8,9},{9,10... | collective-permute-start | bytes 393224 | tf_op jit(solution)/shard_map/ppermute | solution.py:438
  14.1 1.0 copy-start.3
  15.1 0.9 copy-start.4
  16.0 5.2 %copy-start.6 = (f32[4,2,16,256]{3,2,1,0:T(8,128)S(1)}, f32[4,2,16,256]{3,2,1,0:T(8,128)}, u32[]{:S(2)}) copy-start(f32[4,2,16,256]{3,2,1,0:T(8,128)} %param.10) | copy-start | bytes 393220
  17.1 12.2 %copy-start.1 = (bf16[768,384]{1,0:T(8,128)(2,1)S(1)}, bf16[768,384]{1,0:T(8,128)(2,1)}, u32[]{:S(2)}) copy-start(bf16[768,384]{1,0:T(8,128)(2,1)} %constant.18.clone.refs_1_) | copy-start | bytes 1769476
  17.1 12.2 %all-to-all-start = ((f32[8,32,128]{2,1,0:T(8,128)}), f32[8,32,128]{2,1,0:T(8,128)S(1)}, u32[]{:S(2)}, u32[]{:S(2)}) async-start(f32[8,32,128]{2,1,0:T(8,128)} %bitcast.4), calls=%async_computation | async-start | bytes 262144 | tf_op jit(solution)/shard_map/all_to_all | solution.py:455
  21.3 41.4 %collective-permute-start.2 = (f32[3,4,32,256]{3,2,1,0:T(8,128)S(1)}, f32[3,4,32,256]{3,2,1,0:T(8,128)S(1)}, u32[]{:S(2)}, u32[]{:S(2)}) collective-permute-start(f32[3,4,32,256]{3,2,1,0:T(8,128)S(1)} %pad_maximum_fusion), channel_id=1, source_target_pairs={{5,0},{6,1},{7,2},{0,3},{1,4},{2,5},{3,6},{4,7},{13,8},{14,9},{15,... | collective-permute-start | bytes 1179656 | tf_op jit(solution)/shard_map/ppermute | solution.py:438
  30.7 13.4 %copy-start.7 = (s32[2048,6,3]{0,2,1:T(4,128)S(1)}, s32[2048,6,3]{0,2,1:T(4,128)}, u32[]{:S(2)}) copy-start(s32[2048,6,3]{0,2,1:T(4,128)} %param.13) | copy-start | bytes 442372
  30.7 24.5 %all-to-all-start.1 = ((f32[64,4,128]{2,1,0:T(4,128)}), f32[64,4,128]{2,1,0:T(4,128)S(1)}, u32[]{:S(2)}, u32[]{:S(2)}) async-start(f32[64,4,128]{2,1,0:T(4,128)} %bitcast.6), calls=%async_computation.1 | async-start | bytes 262144 | tf_op jit(solution)/shard_map/all_to_all | solution.py:455
  44.2 11.0 %copy-start = (bf16[768,384]{1,0:T(8,128)(2,1)S(1)}, bf16[768,384]{1,0:T(8,128)(2,1)}, u32[]{:S(2)}) copy-start(bf16[768,384]{1,0:T(8,128)(2,1)} %constant.19.clone.refs_5_) | copy-start | bytes 1769476
  45.3 19.9 %collective-permute-start.3 = (f32[2,4,32,256]{3,2,1,0:T(8,128)S(1)}, f32[2,4,32,256]{3,2,1,0:T(8,128)S(1)}, u32[]{:S(2)}, u32[]{:S(2)}) collective-permute-start(f32[2,4,32,256]{3,2,1,0:T(8,128)S(1)} %pad_maximum_fusion.1), channel_id=1, source_target_pairs={{3,0},{4,1},{5,2},{6,3},{7,4},{0,5},{1,6},{2,7},{11,8},{12,9},{13,... | collective-permute-start | bytes 786440 | tf_op jit(solution)/shard_map/ppermute | solution.py:438
  58.2 22.4 %all-to-all-start.2 = ((f32[64,16,128]{2,1,0:T(8,128)}), f32[64,16,128]{2,1,0:T(8,128)S(1)}, u32[]{:S(2)}, u32[]{:S(2)}) async-start(f32[64,16,128]{2,1,0:T(8,128)} %bitcast.8), calls=%async_computation.2 | async-start | bytes 1048576 | tf_op jit(solution)/shard_map/all_to_all | solution.py:455
  65.2 30.6 %collective-permute-start.5 = (f32[8,4,32,256]{3,2,1,0:T(8,128)S(1)}, f32[8,4,32,256]{3,2,1,0:T(8,128)S(1)}, u32[]{:S(2)}, u32[]{:S(2)}) collective-permute-start(f32[8,4,32,256]{3,2,1,0:T(8,128)S(1)} %constant_dynamic-update-slice_fusion.refs_5_), channel_id=1, source_target_pairs={{8,0},{16,8},{24,16},{32,24},{40,32},{48,40},{56,48},{64,56},{72,6... | collective-permute-start | bytes 3145736 | tf_op jit(solution)/shard_map/ppermute | solution.py:438
  68.2 27.7 %collective-permute-start.4 = (f32[8,4,32,256]{3,2,1,0:T(8,128)S(1)}, f32[8,4,32,256]{3,2,1,0:T(8,128)}, u32[]{:S(2)}, u32[]{:S(2)}) collective-permute-start(f32[8,4,32,256]{3,2,1,0:T(8,128)S(1)} %constant_dynamic-update-slice_fusion.refs_5_), channel_id=1, source_target_pairs={{504,0},{0,8},{8,16},{16,24},{24,32},{32,40},{40,48},{48,56},{56,6... | collective-permute-start | bytes 3145736 | tf_op jit(solution)/shard_map/ppermute | solution.py:438
  80.6 15.2 %copy-start.2 = (bf16[1056,256]{1,0:T(8,128)(2,1)S(1)}, bf16[1056,256]{1,0:T(8,128)(2,1)}, u32[]{:S(2)}) copy-start(bf16[1056,256]{1,0:T(8,128)(2,1)} %constant.20.clone.refs_7_) | copy-start | bytes 1622020
  82.0 13.0 %all-to-all-start.3 = ((f32[8,48,128]{2,1,0:T(8,128)}), f32[8,48,128]{2,1,0:T(8,128)S(1)}, u32[]{:S(2)}, u32[]{:S(2)}) async-start(f32[8,48,128]{2,1,0:T(8,128)} %bitcast.10), calls=%async_computation.3 | async-start | bytes 393216 | tf_op jit(solution)/shard_map/all_to_all | solution.py:455
